TPU v7x, 128 devices: a whole 4x4x4 slice. The times are simulated.
128 devices in a mesh: gx: 16 (over x, z_lo, core), gy: 8 (over y, z_hi).
Axes of the slice: x: 4, y: 4, z: 4 (z_hi: 2, z_lo: 2; z = z_hi * 2 + z_lo), core: 2. Of those that a mesh axis runs over, the one named last changes fastest.
Arguments:
- coarse: bfloat16 [128, 64, 32, 64], P(None, 'gx', 'gy'), may hold values from -6 to 6
- skip: bfloat16 [64, 128, 64, 128], P(None, 'gx', 'gy'), may hold values from -6 to 6
- occupancy: int32 [16, 8, 16], P('gx', 'gy'), may hold values 0 or 1
- cotangent: bfloat16 [64, 128, 64, 128], P(None, 'gx', 'gy'), may hold values from -6 to 6
- up_weight: bfloat16 [4, 4, 4, 128, 64], replicated, may hold values from -0.1875 to 0.1875
- conv_weight: bfloat16 [3, 3, 3, 64, 64], replicated, may hold values from -0.15625 to 0.15625
- conv_bias: float32 [64], replicated, may hold values from -3 to 3
Outputs:
- features: bfloat16 [64, 128, 64, 128], P(None, 'gx', 'gy')
- grad_skip: bfloat16 [64, 128, 64, 128], P(None, 'gx', 'gy')
- grad_coarse: bfloat16 [128, 64, 32, 64], P(None, 'gx', 'gy')
- grad_up: float32 [4, 4, 4, 128, 64], replicated
- grad_conv: float32 [3, 3, 3, 64, 64], replicated
- grad_bias: float32 [64], replicated
All inputs are finite; a program needn't handle non-finite values. No bound on the sum of `occupancy` on one device may be relied on, other than what follows from the above.
Results may differ from a plain program's by a relative error of at most 0.0075.
Values may be sent and summed in bfloat16 or wider, within the bound.
A program may use at most 128 MiB of HBM per device.

v0:
```python
import jax
import jax.numpy as jnp
from jax import lax
from jax.sharding import PartitionSpec as P

EDGE = 8


NUMBERS = ("NCDHW", "DHWIO", "NCDHW")
KERNEL_NUMBERS = ("NCDHW", "OIDHW", "NCDHW")


def padded_2(cells, sides, width):
    for axis, dim in sides:
        count = lax.axis_size(axis)
        ends = count - 1
        head = lax.slice_in_dim(cells, 0, width, axis=dim)
        tail = lax.slice_in_dim(cells, cells.shape[dim] - width, cells.shape[dim], axis=dim)
        cells = jnp.concatenate(
            [
                lax.ppermute(tail, axis, [(i, (i + 1) % count) for i in range(ends)]),
                cells,
                lax.ppermute(head, axis, [((i + 1) % count, i) for i in range(ends)]),
            ],
            axis=dim,
        )
    return cells


def spread(occupancy, factor):
    grown = jnp.repeat(occupancy, factor, axis=0)
    grown = jnp.repeat(grown, factor, axis=1)
    return jnp.repeat(grown, factor, axis=2) > 0


def convolve(field, kernel, strides, dilation):
    return lax.conv_general_dilated(
        field[None],
        kernel,
        strides,
        [(0, 0)] * 3,
        lhs_dilation=dilation,
        dimension_numbers=NUMBERS,
        preferred_element_type=jnp.float32,
    )[0]


def kernel_grad(source, target, dilation):
    result = lax.conv_general_dilated(
        source[:, None],
        target[:, None],
        (1, 1, 1),
        [(0, 0)] * 3,
        rhs_dilation=dilation,
        dimension_numbers=KERNEL_NUMBERS,
        preferred_element_type=jnp.float32,
    )
    return result


def depth_pad(field, width):
    return jnp.pad(field, ((0, 0), (0, 0), (0, 0), (width, width)))


def layer(padded, kernel):
    return convolve(padded, kernel, (1, 1, 1), (1, 1, 1))


def body(coarse, skip, occupancy, cotangent, up_weight, conv_weight, conv_bias):
    fine_mask = spread(occupancy, EDGE)
    coarse_mask = spread(occupancy, EDGE // 2)
    active = jnp.where(coarse_mask, coarse, jnp.zeros_like(coarse))
    coarse_pad = padded_2(active, (("gx", 1), ("gy", 2)), 1)
    coarse_pad = depth_pad(coarse_pad, 1)
    upsampled = convolve(coarse_pad, jnp.flip(up_weight, (0, 1, 2)), (1, 1, 1), (2, 2, 2))
    mixed = jnp.where(fine_mask, upsampled + skip.astype(jnp.float32), jnp.float32(0.0)).astype(
        jnp.bfloat16
    )
    mixed_pad = depth_pad(padded_2(mixed, (("gx", 1), ("gy", 2)), 1), 1)
    pre = layer(mixed_pad, conv_weight) + conv_bias[:, None, None, None]
    sig = jax.nn.sigmoid(pre)
    features = jnp.where(fine_mask, pre * sig, jnp.float32(0.0)).astype(jnp.bfloat16)
    slope = sig * (1.0 + pre * (1.0 - sig))
    grad_pre = jnp.where(fine_mask, cotangent.astype(jnp.float32) * slope, jnp.float32(0.0)).astype(
        jnp.bfloat16
    )
    grad_pad = depth_pad(padded_2(grad_pre, (("gx", 1), ("gy", 2)), 1), 1)
    back = layer(grad_pad, jnp.swapaxes(jnp.flip(conv_weight, (0, 1, 2)), 3, 4))
    grad_skip = jnp.where(fine_mask, back, jnp.float32(0.0)).astype(jnp.bfloat16)
    conv_part = jnp.transpose(kernel_grad(mixed_pad, grad_pre, (1, 1, 1)), (2, 3, 4, 0, 1))
    bias_part = jnp.sum(grad_pre.astype(jnp.float32), axis=(1, 2, 3))
    delta_pad = depth_pad(padded_2(grad_skip, (("gx", 1), ("gy", 2)), 1), 1)
    lowered = convolve(delta_pad, jnp.swapaxes(up_weight, 3, 4), (2, 2, 2), (1, 1, 1))
    up_part = jnp.transpose(kernel_grad(delta_pad, active, (2, 2, 2)), (2, 3, 4, 1, 0))
    grad_coarse = jnp.where(coarse_mask, lowered, jnp.float32(0.0)).astype(jnp.bfloat16)
    up_total, conv_total, bias_total = lax.psum((up_part, conv_part, bias_part), ("gx", "gy"))
    scale = float(
        grad_pre.shape[1]
        * lax.axis_size("gx")
        * grad_pre.shape[2]
        * lax.axis_size("gy")
        * grad_pre.shape[3]
    ) ** (-0.5)
    return (
        features,
        grad_skip,
        grad_coarse,
        up_total * scale,
        conv_total * scale,
        bias_total * scale,
    )


def solution(mesh):
    return jax.shard_map(
        body,
        mesh=mesh,
        in_specs=(
            P(None, "gx", "gy", None),
            P(None, "gx", "gy", None),
            P("gx", "gy", None),
            P(None, "gx", "gy", None),
            P(),
            P(),
            P(),
        ),
        out_specs=(
            P(None, "gx", "gy", None),
            P(None, "gx", "gy", None),
            P(None, "gx", "gy", None),
            P(),
            P(),
            P(),
        ),
        check_vma=False,
    )
```

profile of v0, /device:TPU:1, one launch (start us, length us, event | category | flops | bytes accessed | tf_op | source)
XLA Modules:
  0.0 620.4 jit_solution(17170922613313844814)
XLA Ops:
  7.2 0.7 compare_bitcast_fusion
  8.2 1.0 broadcast_select_fusion.2
  9.2 4.9 collective-permute-start
  14.2 1.9 collective-permute-start.1
  16.1 3.6 collective-permute-done.1
  19.8 5.2 collective-permute-start.2
  25.0 1.3 collective-permute-start.3
  27.0 3.2 copy.31
  30.2 1.6 collective-permute-done.3
  32.2 35.1 %fusion.47 = f32[1,64,8,8,128]{1,0,4,3,2:T(1,128)S(1)} fusion(bf16[4,4,4,128,64]{3,4,2,1,0:T(8,128)(2,1)S(1)} %copy-done, bf16[1,128,6,6,66]{1,4,3,2,0:T(8,128)(2,1)S(1)} %fusion.52), kind=kOutput, calls=%fused_computation.65 | convolution fusion | flops 1073741824 | bytes 3753984 | tf_op jit(solution)/shard_map/conv_general_dilated | solution.py:37
  67.3 0.8 select_convert_fusion.2
  68.2 2.7 collective-permute-start.4
  70.9 1.9 collective-permute-start.5
  72.8 1.4 collective-permute-done.4
  74.2 4.4 collective-permute-done.5
  78.6 0.7 copy-done.8
  79.3 1.0 pad_maximum_fusion.8
  80.3 5.7 collective-permute-start.6
  85.9 1.5 collective-permute-start.7
  87.4 3.2 copy.36
  90.7 5.9 collective-permute-done.6
  96.5 5.0 fusion.82
  101.6 2.5 pad.18
  104.1 7.1 %reshape.33 = bf16[64,10,10,1,8,17]{0,5,4,2,1,3:T(8,128)(2,1)} reshape(bf16[64,10,10,1,136]{0,4,2,1,3:T(8,128)(2,1)} %pad.18) | data formatting | bytes 3481600 | tf_op jit(solution)/shard_map/conv_general_dilated | solution.py:37
  111.2 3.1 copy.33
  114.4 144.2 %broadcast_select_fusion.1 = f32[8,8,8,17,64]{4,2,3,1,0:T(8,128)S(1)} fusion(pred[8,17]{0,1:T(8,128)(4,1)S(1)} %copy-done.25, bf16[3,3,3,64,64]{4,3,2,1,0:T(8,128)(2,1)S(1)} %copy-done.23, bf16[64,10,10,1,7,2]{0,4,5,2,1,3:T(8,128)(2,1)S(1)} %slice.74, bf16[64,10,10,1,8,17]{0,4,5,2,1,3:T(8,128)(2,1)S(1)} %copy.33), kind=kOutput, calls=%fused_computation.58 | convolution fusion | flops 1931579392 | bytes 4369544 | tf_op jit(solution)/shard_map/conv_general_dilated | solution.py:37
  258.6 0.8 copy.34
  259.7 1.3 copy-done.6
  261.0 4.2 convert_reduce_fusion
  265.2 3.2 collective-permute-start.8
  268.4 1.9 collective-permute-start.9
  270.3 1.4 collective-permute-done.8
  271.7 5.3 collective-permute-done.9
  277.1 5.9 collective-permute-start.10
  283.0 1.7 collective-permute-start.11
  284.7 0.8 fusion.81
  285.5 8.9 %collective-permute-done.10 = bf16[64,10,1,128]{0,3,2,1:T(8,128)(2,1)S(1)} collective-permute-done((bf16[64,10,1,128]{0,3,2,1:T(8,128)(2,1)S(1)}, bf16[64,10,1,128]{0,3,2,1:T(8,128)(2,1)S(1)}, u32[]{:S(2)}, u32[]{:S(2)}) %collective-permute-start.10) | collective-permute-done | bytes 163872 | tf_op jit(solution)/shard_map/ppermute | solution.py:21
  294.5 3.1 fusion.33
  297.6 2.5 pad.20
  300.1 7.1 %reshape.40 = bf16[64,10,10,1,8,17]{0,5,4,2,1,3:T(8,128)(2,1)} reshape(bf16[64,10,10,1,136]{0,4,2,1,3:T(8,128)(2,1)} %pad.20) | data formatting | bytes 3481600 | tf_op jit(solution)/shard_map/conv_general_dilated | solution.py:37
  307.2 3.1 copy.38
  310.4 16.1 %broadcast_select_fusion = bf16[8,8,8,17,64]{4,2,3,1,0:T(8,128)(2,1)S(1)} fusion(pred[8,17]{0,1:T(8,128)(4,1)S(1)} %copy-done.25, bf16[3,3,3,64,64]{4,3,2,1,0:T(8,128)(2,1)S(1)} %copy-done.24, bf16[64,10,10,1,7,2]{0,4,5,2,1,3:T(8,128)(2,1)S(1)} %slice.78, bf16[64,10,10,1,8,17]{0,4,5,2,1,3:T(8,128)(2,1)S(1)} %copy.38), kind=kOutput, calls=%fused_computation.57 | convolution fusion | flops 1931579392 | bytes 3255432 | tf_op jit(solution)/shard_map/conv_general_dilated | solution.py:37
  327.0 0.7 fusion.16
  327.7 1.9 collective-permute-start.12
  329.7 2.5 collective-permute-start.13
  332.2 4.1 fusion.80
  336.4 3.5 collective-permute-done.13
  339.8 1.0 pad_maximum_fusion.2
  340.8 7.3 %collective-permute-start.14 = (bf16[64,10,1,128]{0,3,2,1:T(8,128)(2,1)}, bf16[64,10,1,128]{0,3,2,1:T(8,128)(2,1)}, u32[]{:S(2)}, u32[]{:S(2)}) collective-permute-start(bf16[64,10,1,128]{0,3,2,1:T(8,128)(2,1)} %get-tuple-element.25), channel_id=1, source_target_pairs={{0,1},{1,2},{2,3},{3,4},{4,5},{5,6},{6,7},{8,9},{9,10},{10,11},{11... | collective-permute-start | bytes 491528 | tf_op jit(solution)/shard_map/ppermute | solution.py:21
  348.1 1.3 collective-permute-start.15
  349.5 63.5 %fusion.6 = f32[3,3,3,64,64]{4,3,2,1,0:T(8,128)} fusion(bf16[64,1,10,10,130]{0,4,3,2,1:T(8,128)(2,1)S(1)} %fusion.80, bf16[64,1,8,8,128]{0,4,3,2,1:T(8,128)(2,1)S(1)} %bitcast.79), kind=kOutput, calls=%fused_computation.10 | convolution fusion | flops 1811939328 | bytes 3154944 | tf_op jit(solution)/shard_map/transpose | solution.py:90
  413.0 5.4 fusion.71
  418.4 27.9 %fusion.4 = f32[4,4,4,128,64]{3,4,2,1,0:T(8,128)} fusion(bf16[64,1,10,10,130]{0,4,3,2,1:T(8,128)(2,1)S(1)} %get-tuple-element.23, bf16[128,1,4,4,64]{0,4,3,2,1:T(8,128)(2,1)S(1)} %copy-done.16), kind=kOutput, calls=%fused_computation.8 | convolution fusion | flops 1073741824 | bytes 4023296 | tf_op jit(solution)/shard_map/transpose | solution.py:94
  446.3 3.6 copy.49
  449.9 76.3 %psum.23 = f32[64]{0:T(128)S(1)} all-reduce(f32[64]{0:T(128)S(1)} %copy-done.22), channel_id=1, replica_groups=mesh['gx'=16,'gy'=8] {'gx','gy'}, use_global_device_ids=true, to_apply=%region_3.4 | all-reduce | flops 64 | bytes 512 | tf_op jit(solution)/shard_map/psum | solution.py:96
  526.7 2.3 copy.50
  529.0 4.6 pad.22
  533.6 7.0 %reshape.47 = bf16[64,10,10,1,8,18]{0,5,4,2,1,3:T(8,128)(2,1)} reshape(bf16[64,10,10,1,144]{0,4,2,1,3:T(8,128)(2,1)} %pad.22) | data formatting | bytes 3686400 | tf_op jit(solution)/shard_map/conv_general_dilated | solution.py:37
  540.6 3.1 copy.42
  543.9 2.7 fusion.49
  546.8 0.8 fusion.59
  547.6 61.2 %all-reduce.7.cloned.1.call-done = (f32[4,4,4,128,64]{3,4,2,1,0:T(8,128)}, f32[3,3,3,64,64]{4,3,2,1,0:T(8,128)}) async-done(((f32[4,4,4,128,64]{3,4,2,1,0:T(8,128)}, f32[3,3,3,64,64]{4,3,2,1,0:T(8,128)}), (f32[4,4,4,128,64]{3,4,2,1,0:T(8,128)}, f32[3,3,3,64,64]{4,3,2,1,0:T(8,128)})) %all-reduce.7.cloned.1.call-update) | async-done | bytes 2539536 | tf_op jit(solution)/shard_map/psum | solution.py:96
  608.9 3.3 broadcast_multiply_fusion
  612.2 1.0 broadcast_multiply_fusion.1
  (81 shorter events, 3.4 us)
Async XLA Ops:
  7.2 25.0 %copy-start = (bf16[4,4,4,128,64]{3,4,2,1,0:T(8,128)(2,1)S(1)}, bf16[4,4,4,128,64]{3,4,2,1,0:T(8,128)(2,1)}, u32[]{:S(2)}) copy-start(bf16[4,4,4,128,64]{3,4,2,1,0:T(8,128)(2,1)} %param.11) | copy-start | bytes 3145732
  7.2 601.7 %all-reduce.7.cloned.1.call-start = ((), (), s32[]{:S(2)}) async-start(), calls=%async_computation | async-start | bytes 5963776 | tf_op jit(solution)/shard_map/psum | solution.py:96
  8.1 1.1 copy-start.17
  9.2 6.9 %collective-permute-start = (bf16[128,1,4,64]{0,3,2,1:T(8,128)(2,1)S(1)}, bf16[128,1,4,64]{0,3,2,1:T(8,128)(2,1)S(1)}, u32[]{:S(2)}, u32[]{:S(2)}) collective-permute-start(bf16[128,1,4,64]{0,3,2,1:T(8,128)(2,1)S(1)} %get-tuple-element.39), channel_id=1, source_target_pairs={{0,8},{8,16},{16,24},{24,32},{32,40},{40,48},{48,56},{56,64},{64,7... | collective-permute-start | bytes 196616 | tf_op jit(solution)/shard_map/ppermute | solution.py:21
  14.2 5.6 collective-permute-start.1
  19.8 10.4 %collective-permute-start.2 = (bf16[128,6,1,64]{0,3,2,1:T(8,128)(2,1)S(1)}, bf16[128,6,1,64]{0,3,2,1:T(8,128)(2,1)S(1)}, u32[]{:S(2)}, u32[]{:S(2)}) collective-permute-start(bf16[128,6,1,64]{0,3,2,1:T(8,128)(2,1)S(1)} %get-tuple-element.37), channel_id=1, source_target_pairs={{0,1},{1,2},{2,3},{3,4},{4,5},{5,6},{6,7},{8,9},{9,10},{10,11},{11... | collective-permute-start | bytes 294920 | tf_op jit(solution)/shard_map/ppermute | solution.py:21
  25.0 6.9 %collective-permute-start.3 = (bf16[128,6,1,64]{0,3,2,1:T(8,128)(2,1)S(1)}, bf16[128,6,1,64]{0,3,2,1:T(8,128)(2,1)S(1)}, u32[]{:S(2)}, u32[]{:S(2)}) collective-permute-start(bf16[128,6,1,64]{0,3,2,1:T(8,128)(2,1)S(1)} %get-tuple-element.38), channel_id=1, source_target_pairs={{1,0},{2,1},{3,2},{4,3},{5,4},{6,5},{7,6},{9,8},{10,9},{11,10},{12... | collective-permute-start | bytes 294920 | tf_op jit(solution)/shard_map/ppermute | solution.py:23
  32.2 35.1 %copy-start.7 = (bf16[64,8,8,128]{0,3,2,1:T(8,128)(2,1)S(1)}, bf16[64,8,8,128]{0,3,2,1:T(8,128)(2,1)}, u32[]{:S(2)}) copy-start(bf16[64,8,8,128]{0,3,2,1:T(8,128)(2,1)} %copy.31) | copy-start | bytes 3145732
  32.2 35.1 %copy-start.20 = (pred[128]{0:T(512)(128)(4,1)S(1)}, pred[128]{0:T(512)(128)(4,1)}, u32[]{:S(2)}) copy-start(pred[128]{0:T(512)(128)(4,1)} %gt.25) | copy-start | bytes 388
  68.2 6.0 collective-permute-start.4
  70.9 7.7 %collective-permute-start.5 = (bf16[64,1,8,128]{0,3,2,1:T(8,128)(2,1)S(1)}, bf16[64,1,8,128]{0,3,2,1:T(8,128)(2,1)S(1)}, u32[]{:S(2)}, u32[]{:S(2)}) collective-permute-start(bf16[64,1,8,128]{0,3,2,1:T(8,128)(2,1)S(1)} %get-tuple-element.36), channel_id=1, source_target_pairs={{8,0},{16,8},{24,16},{32,24},{40,32},{48,40},{56,48},{64,56},{72,6... | collective-permute-start | bytes 393224 | tf_op jit(solution)/shard_map/ppermute | solution.py:23
  78.6 0.7 copy-start.8
  80.3 16.3 %collective-permute-start.6 = (bf16[64,10,1,128]{0,3,2,1:T(8,128)(2,1)}, bf16[64,10,1,128]{0,3,2,1:T(8,128)(2,1)}, u32[]{:S(2)}, u32[]{:S(2)}) collective-permute-start(bf16[64,10,1,128]{0,3,2,1:T(8,128)(2,1)} %get-tuple-element.29), channel_id=1, source_target_pairs={{0,1},{1,2},{2,3},{3,4},{4,5},{5,6},{6,7},{8,9},{9,10},{10,11},{11... | collective-permute-start | bytes 491528 | tf_op jit(solution)/shard_map/ppermute | solution.py:21
  85.9 10.6 %collective-permute-start.7 = (bf16[64,10,1,128]{0,3,2,1:T(8,128)(2,1)}, bf16[64,10,1,128]{0,3,2,1:T(8,128)(2,1)}, u32[]{:S(2)}, u32[]{:S(2)}) collective-permute-start(bf16[64,10,1,128]{0,3,2,1:T(8,128)(2,1)} %get-tuple-element.30), channel_id=1, source_target_pairs={{1,0},{2,1},{3,2},{4,3},{5,4},{6,5},{7,6},{9,8},{10,9},{11,10},{12... | collective-permute-start | bytes 491528 | tf_op jit(solution)/shard_map/ppermute | solution.py:23
  111.2 3.2 copy-start.23
  111.2 3.2 copy-start.25
  259.4 1.6 copy-start.6
  259.4 1.6 copy-start.21
  265.1 29.3 %copy-start.4 = (bf16[64,8,8,128]{0,3,2,1:T(8,128)(2,1)}, bf16[64,8,8,128]{0,3,2,1:T(8,128)(2,1)S(1)}, u32[]{:S(2)}) copy-start(bf16[64,8,8,128]{0,3,2,1:T(8,128)(2,1)S(1)} %get-tuple-element.21) | copy-start | bytes 3145732
  265.1 19.6 %copy-start.14 = (bf16[128,4,4,64]{0,3,2,1:T(8,128)(2,1)S(1)}, bf16[128,4,4,64]{0,3,2,1:T(8,128)(2,1)}, u32[]{:S(2)}) copy-start(bf16[128,4,4,64]{0,3,2,1:T(8,128)(2,1)} %param.7) | copy-start | bytes 786436
  265.1 19.6 %copy-start.18 = (pred[64]{0:T(512)(128)(4,1)S(1)}, pred[64]{0:T(512)(128)(4,1)}, u32[]{:S(2)}) copy-start(pred[64]{0:T(512)(128)(4,1)} %copy-done.17) | copy-start | bytes 196
  265.2 6.5 %collective-permute-start.8 = (bf16[64,1,8,128]{0,3,2,1:T(8,128)(2,1)S(1)}, bf16[64,1,8,128]{0,3,2,1:T(8,128)(2,1)S(1)}, u32[]{:S(2)}, u32[]{:S(2)}) collective-permute-start(bf16[64,1,8,128]{0,3,2,1:T(8,128)(2,1)S(1)} %get-tuple-element.33), channel_id=1, source_target_pairs={{0,8},{8,16},{16,24},{24,32},{32,40},{40,48},{48,56},{56,64},{64,7... | collective-permute-start | bytes 393224 | tf_op jit(solution)/shard_map/ppermute | solution.py:21
  268.4 8.5 %collective-permute-start.9 = (bf16[64,1,8,128]{0,3,2,1:T(8,128)(2,1)S(1)}, bf16[64,1,8,128]{0,3,2,1:T(8,128)(2,1)S(1)}, u32[]{:S(2)}, u32[]{:S(2)}) collective-permute-start(bf16[64,1,8,128]{0,3,2,1:T(8,128)(2,1)S(1)} %get-tuple-element.34), channel_id=1, source_target_pairs={{8,0},{16,8},{24,16},{32,24},{40,32},{48,40},{56,48},{64,56},{72,6... | collective-permute-start | bytes 393224 | tf_op jit(solution)/shard_map/ppermute | solution.py:23
  277.1 17.4 %collective-permute-start.10 = (bf16[64,10,1,128]{0,3,2,1:T(8,128)(2,1)S(1)}, bf16[64,10,1,128]{0,3,2,1:T(8,128)(2,1)S(1)}, u32[]{:S(2)}, u32[]{:S(2)}) collective-permute-start(bf16[64,10,1,128]{0,3,2,1:T(8,128)(2,1)S(1)} %get-tuple-element.27), channel_id=1, source_target_pairs={{0,1},{1,2},{2,3},{3,4},{4,5},{5,6},{6,7},{8,9},{9,10},{10,11},{11... | collective-permute-start | bytes 491528 | tf_op jit(solution)/shard_map/ppermute | solution.py:21
  283.0 11.5 %collective-permute-start.11 = (bf16[64,10,1,128]{0,3,2,1:T(8,128)(2,1)S(1)}, bf16[64,10,1,128]{0,3,2,1:T(8,128)(2,1)S(1)}, u32[]{:S(2)}, u32[]{:S(2)}) collective-permute-start(bf16[64,10,1,128]{0,3,2,1:T(8,128)(2,1)S(1)} %get-tuple-element.28), channel_id=1, source_target_pairs={{1,0},{2,1},{3,2},{4,3},{5,4},{6,5},{7,6},{9,8},{10,9},{11,10},{12... | collective-permute-start | bytes 491528 | tf_op jit(solution)/shard_map/ppermute | solution.py:23
  307.2 3.2 copy-start.24
  326.8 5.4 copy-start.9
  327.7 12.2 %copy-start.1 = (bf16[64,8,8,128]{0,3,2,1:T(8,128)(2,1)}, bf16[64,8,8,128]{0,3,2,1:T(8,128)(2,1)S(1)}, u32[]{:S(2)}) copy-start(bf16[64,8,8,128]{0,3,2,1:T(8,128)(2,1)S(1)} %fusion.16) | copy-start | bytes 3145732
  327.7 8.6 %collective-permute-start.12 = (bf16[64,1,8,128]{0,3,2,1:T(8,128)(2,1)S(1)}, bf16[64,1,8,128]{0,3,2,1:T(8,128)(2,1)S(1)}, u32[]{:S(2)}, u32[]{:S(2)}) collective-permute-start(bf16[64,1,8,128]{0,3,2,1:T(8,128)(2,1)S(1)} %get-tuple-element.31), channel_id=1, source_target_pairs={{0,8},{8,16},{16,24},{24,32},{32,40},{40,48},{48,56},{56,64},{64,7... | collective-permute-start | bytes 393224 | tf_op jit(solution)/shard_map/ppermute | solution.py:21
  329.6 19.8 %copy-start.5 = (bf16[64,8,8,128]{0,3,2,1:T(8,128)(2,1)S(1)}, bf16[64,8,8,128]{0,3,2,1:T(8,128)(2,1)}, u32[]{:S(2)}) copy-start(bf16[64,8,8,128]{0,3,2,1:T(8,128)(2,1)} %copy-done.4) | copy-start | bytes 3145732
  329.7 10.2 %collective-permute-start.13 = (bf16[64,1,8,128]{0,3,2,1:T(8,128)(2,1)S(1)}, bf16[64,1,8,128]{0,3,2,1:T(8,128)(2,1)S(1)}, u32[]{:S(2)}, u32[]{:S(2)}) collective-permute-start(bf16[64,1,8,128]{0,3,2,1:T(8,128)(2,1)S(1)} %get-tuple-element.32), channel_id=1, source_target_pairs={{8,0},{16,8},{24,16},{32,24},{40,32},{48,40},{56,48},{64,56},{72,6... | collective-permute-start | bytes 393224 | tf_op jit(solution)/shard_map/ppermute | solution.py:23
  336.4 13.1 %copy-start.10 = (bf16[64,1,8,128]{0,3,2,1:T(8,128)(2,1)}, bf16[64,1,8,128]{0,3,2,1:T(8,128)(2,1)S(1)}, u32[]{:S(2)}) copy-start(bf16[64,1,8,128]{0,3,2,1:T(8,128)(2,1)S(1)} %collective-permute-done.12) | copy-start | bytes 393220
  339.8 9.6 %copy-start.12 = (bf16[64,1,8,128]{0,3,2,1:T(8,128)(2,1)}, bf16[64,1,8,128]{0,3,2,1:T(8,128)(2,1)S(1)}, u32[]{:S(2)}) copy-start(bf16[64,1,8,128]{0,3,2,1:T(8,128)(2,1)S(1)} %collective-permute-done.13) | copy-start | bytes 393220
  340.8 72.1 %collective-permute-start.14 = (bf16[64,10,1,128]{0,3,2,1:T(8,128)(2,1)}, bf16[64,10,1,128]{0,3,2,1:T(8,128)(2,1)}, u32[]{:S(2)}, u32[]{:S(2)}) collective-permute-start(bf16[64,10,1,128]{0,3,2,1:T(8,128)(2,1)} %get-tuple-element.25), channel_id=1, source_target_pairs={{0,1},{1,2},{2,3},{3,4},{4,5},{5,6},{6,7},{8,9},{9,10},{10,11},{11... | collective-permute-start | bytes 491528 | tf_op jit(solution)/shard_map/ppermute | solution.py:21
  348.1 64.9 %collective-permute-start.15 = (bf16[64,10,1,128]{0,3,2,1:T(8,128)(2,1)}, bf16[64,10,1,128]{0,3,2,1:T(8,128)(2,1)}, u32[]{:S(2)}, u32[]{:S(2)}) collective-permute-start(bf16[64,10,1,128]{0,3,2,1:T(8,128)(2,1)} %get-tuple-element.26), channel_id=1, source_target_pairs={{1,0},{2,1},{3,2},{4,3},{5,4},{6,5},{7,6},{9,8},{10,9},{11,10},{12... | collective-permute-start | bytes 491528 | tf_op jit(solution)/shard_map/ppermute | solution.py:23
  349.4 63.5 %copy-start.2 = (bf16[64,8,8,128]{0,3,2,1:T(8,128)(2,1)S(1)}, bf16[64,8,8,128]{0,3,2,1:T(8,128)(2,1)}, u32[]{:S(2)}) copy-start(bf16[64,8,8,128]{0,3,2,1:T(8,128)(2,1)} %copy-done.1) | copy-start | bytes 3145732
  349.5 63.5 %copy-start.11 = (bf16[64,1,8,128]{0,3,2,1:T(8,128)(2,1)S(1)}, bf16[64,1,8,128]{0,3,2,1:T(8,128)(2,1)}, u32[]{:S(2)}) copy-start(bf16[64,1,8,128]{0,3,2,1:T(8,128)(2,1)} %copy-done.10) | copy-start | bytes 393220
  349.5 63.5 %copy-start.13 = (bf16[64,1,8,128]{0,3,2,1:T(8,128)(2,1)S(1)}, bf16[64,1,8,128]{0,3,2,1:T(8,128)(2,1)}, u32[]{:S(2)}) copy-start(bf16[64,1,8,128]{0,3,2,1:T(8,128)(2,1)} %copy-done.12) | copy-start | bytes 393220
  413.0 5.4 copy-start.16
  446.3 3.6 copy-start.22
  446.3 80.4 %copy-start.3 = (bf16[64,8,8,128]{0,3,2,1:T(8,128)(2,1)S(1)}, bf16[64,8,8,128]{0,3,2,1:T(8,128)(2,1)}, u32[]{:S(2)}) copy-start(bf16[64,8,8,128]{0,3,2,1:T(8,128)(2,1)} %copy-done.1) | copy-start | bytes 3145732
  540.6 3.3 copy-start.26
  543.9 2.9 copy-start.19
  608.9 3.3 copy-start.15
Sparse Core Ops, SparseCore 0:
  446.4 162.3 all-reduce.6
where the time goes:
time: 630 us; the launch traced here: 620 us
  matrix products  289 us (46%)
  waiting for transfers between devices  97.2 us (15%)
  blocking collectives  76.3 us (12%)
  local copies, waits for them, and re-layouts  57.5 us (9%)
  starting transfers between devices  50.9 us (8%)
  other arithmetic  34 us (5%)
  between operations  15.1 us (2%)
    conv_general_dilated x4, matrix products, convolve(): lax.conv_general_dilated(field[None], kernel, strides, [(0, 0)] * 3, lhs_...  198 us
    psum x1, blocking collectives, body(): lax.psum((up_part, conv_part, bias_part), ('gx', 'gy'))  76.3 us
    transpose x1, matrix products, body(): jnp.transpose(kernel_grad(mixed_pad, grad_pre, (1, 1, 1)), (2, 3, 4, 0, 1))  63.5 us
    psum x1, waiting for transfers between devices, body(): lax.psum((up_part, conv_part, bias_part), ('gx', 'gy'))  61.2 us
    ppermute x8, starting transfers between devices, padded_2(): lax.ppermute(tail, axis, [(i, (i + 1) % count) for i in range(ends)])  36.8 us
    conv_general_dilated x15, local copies, waits for them, and re-layouts, convolve(): lax.conv_general_dilated(field[None], kernel, strides, [(0, 0)] * 3, lhs_...  32.5 us
    transpose x1, matrix products, body(): jnp.transpose(kernel_grad(delta_pad, active, (2, 2, 2)), (2, 3, 4, 1, 0))  27.9 us
    ppermute x8, waiting for transfers between devices, padded_2(): lax.ppermute(head, axis, [((i + 1) % count, i) for i in range(ends)])  18.4 us
  transfers between devices with their start and end apart: 17, of which 10 were waited for; matrix products, arithmetic and copies ran while one was open for 16% of the time, Pallas kernels for 0%

commit v1 on v0

v1 whole, which is shorter than its diff:
```python
import jax
import jax.numpy as jnp
from jax import lax
from jax.experimental import pallas as pl
from jax.experimental.pallas import tpu as pltpu
from jax.sharding import PartitionSpec as P

BF = jnp.bfloat16
F32 = jnp.float32
EDGE = 8
MESH = pl.DeviceIdType.MESH
VMEM = pl.BlockSpec(memory_space=pltpu.VMEM)
LIMIT = 56 * 2**20

U_ROWS = 4096
C_ROWS = 592
ROWS = 6144


def mm(a, b):
    return lax.dot_general(a, b, (((1,), (0,)), ((), ())), preferred_element_type=F32)


def mm_t(a, b):
    return lax.dot_general(a, b, (((1,), (1,)), ((), ())), preferred_element_type=F32)


def lanes(parts):
    return jnp.concatenate(parts, axis=1)


def call(body, out, scratch=(), collective=None):
    extra = {} if collective is None else {"collective_id": collective, "has_side_effects": True}
    return pl.pallas_call(
        body,
        out_shape=out,
        scratch_shapes=list(scratch),
        compiler_params=pltpu.CompilerParams(vmem_limit_bytes=LIMIT, **extra),
    )


def shape(dims, kind=BF):
    return jax.ShapeDtypeStruct(dims, kind)


AROUND = [(1, 0), (-1, 0), (0, 1), (0, -1), (1, 1), (1, -1), (-1, 1), (-1, -1)]


def neighbour(dx, dy):
    nx, ny = lax.axis_size("gx"), lax.axis_size("gy")
    gx, gy = lax.axis_index("gx"), lax.axis_index("gy")
    return lax.rem(gx + (dx + nx), nx), lax.rem(gy + (dy + ny), ny)


def greet_around():
    barrier = pltpu.get_barrier_semaphore()
    for dx, dy in AROUND:
        pl.semaphore_signal(barrier, inc=1, device_id=neighbour(dx, dy), device_id_type=MESH)
    pl.semaphore_wait(barrier, len(AROUND))


def edge(step, count):
    if step == 0:
        return pl.ds(0, count), pl.ds(1, count)
    if step > 0:
        return pl.ds(count - 1, 1), pl.ds(0, 1)
    return pl.ds(0, 1), pl.ds(count + 1, 1)


def halo_copies(block, field, send, recv, first):
    copies = []
    for at, (dx, dy) in enumerate(AROUND):
        sx, tx = edge(dx, block.shape[0])
        sy, ty = edge(dy, block.shape[1])
        copies.append(
            pltpu.make_async_remote_copy(
                src_ref=block.at[sx, sy],
                dst_ref=field.at[tx, ty],
                send_sem=send.at[first + at],
                recv_sem=recv.at[first + at],
                device_id=neighbour(dx, dy),
                device_id_type=MESH,
            )
        )
    return copies


def fill_middle(block, field):
    across, along = block.shape[0], block.shape[1]

    def row(x, carry):
        field[x + 1, pl.ds(1, along)] = block[x]
        return carry

    lax.fori_loop(0, across, row, 0)


def clear_outside(field):
    across, along = field.shape[0], field.shape[1]
    nx, ny = lax.axis_size("gx"), lax.axis_size("gy")
    gx, gy = lax.axis_index("gx"), lax.axis_index("gy")
    row = jnp.zeros((1,) + field.shape[1:], field.dtype)
    column = jnp.zeros((across, 1) + field.shape[2:], field.dtype)

    @pl.when(gx == 0)
    def _():
        field[0:1] = row

    @pl.when(gx == nx - 1)
    def _():
        field[across - 1 : across] = row

    @pl.when(gy == 0)
    def _():
        field[:, 0:1] = column

    @pl.when(gy == ny - 1)
    def _():
        field[:, along - 1 : along] = column


def exchange_body(*refs):
    count = (len(refs) - 2) // 2
    blocks, fields = refs[:count], refs[count : 2 * count]
    send, recv = refs[2 * count :]
    greet_around()
    copies = []
    for at in range(count):
        copies += halo_copies(blocks[at], fields[at], send, recv, at * len(AROUND))
    for copy in copies:
        copy.start()
    for at in range(count):
        fill_middle(blocks[at], fields[at])
    for copy in copies:
        copy.wait()
    for at in range(count):
        clear_outside(fields[at])


def exchange(blocks, collective):
    outs = [shape((b.shape[0] + 2, b.shape[1] + 2) + b.shape[2:], b.dtype) for b in blocks]
    sems = [pltpu.SemaphoreType.DMA((len(AROUND) * len(blocks),))] * 2
    return call(exchange_body, outs, sems, collective)(*blocks)


def lane_of(dims):
    return lax.broadcasted_iota(jnp.int32, dims, len(dims) - 1)


def conv_window(field, i, y):
    return jnp.concatenate(
        [
            lanes(
                [
                    field[i + 4 * h + k, pl.ds(y + e, 3)].reshape(192, 128)
                    for e in range(2)
                    for h in range(2)
                ]
            )
            for k in range(3)
        ],
        axis=0,
    )


def join_taps(taps, lane):
    back = jnp.where(lane == 0, 0.0, pltpu.roll(taps[0:64], 1, 1))
    ahead = jnp.where(lane == 127, 0.0, pltpu.roll(taps[128:192], 127, 1))
    return taps[64:128] + back + ahead


def front_body(
    sf, cf, cot, wu, wc, bias, spread_up, widen, feat, gp, ac, gconv, mx, g3, masks, gacc
):
    lane = lane_of((64, 128))
    for dx in range(3):
        for dy in range(3):
            row = cf[(0, 1, 5)[dx], (0, 1, 5)[dy], 0:16]
            masks[dx, dy] = mm(row, widen[...])

    def pair_coarse(t, carry):
        i, y = t // 6, t % 6
        left = cf[i, y].astype(F32)
        right = pltpu.roll(cf[i + 2, y].astype(F32), 64, 1)
        ac[i, y] = jnp.where(lane_of((128, 128)) < 64, left, right).astype(BF)
        return carry

    lax.fori_loop(0, 24, pair_coarse, 0)

    def mask_of(x, y):
        bx = jnp.where(x == 0, 0, jnp.where(x == 9, 2, 1))
        by = jnp.where(y == 0, 0, jnp.where(y == 9, 2, 1))
        return masks[bx, by, 0:1, :] > 0.5

    def mix(p, q, taps):
        wide = jnp.concatenate(
            [
                lanes([taps[(s * 4 + kz) * 64 : (s * 4 + kz + 1) * 64] for kz in range(4)])
                for s in range(4)
            ],
            axis=0,
        )
        up = mm(wide, spread_up[...])
        for s in range(4):
            for h in range(2):
                x = 2 * p + s // 2 + 4 * h
                y = 2 * q + s % 2
                value = up[s * 64 : s * 64 + 64, h * 128 : h * 128 + 128] + sf[x, y].astype(F32)
                mx[x, y] = jnp.where(mask_of(x, y), value, 0.0).astype(BF)

    def up_pair(t, carry):
        p, q = t // 2, (t % 2) * 2
        window = lanes([ac[pl.ds(p, 2), pl.ds(q + e, 2)].reshape(512, 128) for e in range(2)])
        taps = mm(wu[...], window).astype(BF)
        for e in range(2):
            mix(p, q + e, taps[:, e * 128 : e * 128 + 128])
        return carry

    lax.fori_loop(0, 6, up_pair, 0)

    def up_last(p, carry):
        taps = mm(wu[...], ac[pl.ds(p, 2), pl.ds(4, 2)].reshape(512, 128)).astype(BF)
        mix(p, 4, taps)
        return carry

    lax.fori_loop(0, 3, up_last, 0)

    inside = masks[1, 1, 0:1, :] > 0.5

    def conv(t, carry):
        i, y = t // 4, (t % 4) * 2
        taps = mm(wc[...], conv_window(mx, i, y))
        for e in range(2):
            for h in range(2):
                at = (e * 2 + h) * 128
                pre = join_taps(taps[:, at : at + 128], lane) + bias[...]
                sig = 1.0 / (1.0 + jnp.exp(-pre))
                feat[i + 4 * h, y + e] = jnp.where(inside, pre * sig, 0.0).astype(BF)
                slope = sig * (1.0 + pre * (1.0 - sig))
                grad = cot[i + 4 * h, y + e].astype(F32) * slope
                grad = jnp.where(inside, grad, 0.0).astype(BF)
                gp[i + 4 * h, y + e] = grad
                wide = grad.astype(F32)
                before = jnp.where(lane == 127, 0.0, pltpu.roll(wide, 127, 1)).astype(BF)
                after = jnp.where(lane == 0, 0.0, pltpu.roll(wide, 1, 1)).astype(BF)
                g3[i, y + e, :, h * 128 : h * 128 + 128] = jnp.concatenate(
                    [before, grad, after], axis=0
                )
        return carry

    lax.fori_loop(0, 16, conv, 0)

    gacc[...] = jnp.zeros_like(gacc)

    def kernel_grad(t, carry):
        i, y = t // 2, (t % 2) * 4
        grads = lanes([g3[i, y + j] for j in range(4)])
        for k in range(3):
            cells = lanes(
                [
                    mx[i + 4 * h + k, pl.ds(y + j, 3)].reshape(192, 128)
                    for j in range(4)
                    for h in range(2)
                ]
            )
            gacc[k * 192 : k * 192 + 192, :] += mm_t(cells, grads)
        gacc[576:592, :] += mm_t(jnp.ones((16, 1024), BF), grads)
        return carry

    lax.fori_loop(0, 8, kernel_grad, 0)
    gconv[0:592, :] = gacc[:, 0:128].astype(BF)
    gconv[592:1184, 0:64] = gacc[:, 128:192].astype(BF)
    gconv[592:1184, 64:128] = jnp.zeros((592, 64), BF)


def back_body(gpf, ac, wb, gather_z, mask, gs, gup, d4):
    lane = lane_of((64, 128))
    inside = mask[0:1, :] > 0.5

    def conv(t, carry):
        i, y = t // 4, (t % 4) * 2
        taps = mm(wb[...], conv_window(gpf, i, y))
        for e in range(2):
            both = []
            for h in range(2):
                at = (e * 2 + h) * 128
                grad = join_taps(taps[:, at : at + 128], lane)
                grad = jnp.where(inside, grad, 0.0).astype(BF)
                gs[i + 4 * h, y + e] = grad
                both.append(grad)
            apart = mm(lanes(both), gather_z[...]).astype(BF)
            for kz in range(4):
                d4[i, y + e, kz * 64 : kz * 64 + 64, :] = apart[:, kz * 128 : kz * 128 + 128]
        return carry

    lax.fori_loop(0, 16, conv, 0)

    for sx in range(2):
        for sy in range(2):
            spots = [
                (pi, qi)
                for pi in range(1 - sx, 3 - sx)
                for qi in range(1 - sy, 5 - sy)
            ]
            grads = lanes([d4[2 * pi - 1 + sx, 2 * qi - 1 + sy] for pi, qi in spots])
            cells = jnp.concatenate(
                [
                    lanes([ac[pi + tx, qi + ty] for pi, qi in spots])
                    for tx in range(2)
                    for ty in range(2)
                ],
                axis=0,
            )
            total = mm_t(cells, grads).astype(BF)
            for tx in range(2):
                for ty in range(2):
                    tap = (2 + sx - 2 * tx) * 4 + 2 + sy - 2 * ty
                    rows = (tx * 2 + ty) * 128
                    for half in range(2):
                        at = (tap * 2 + half) * 128
                        gup[at : at + 128, :] = total[
                            rows : rows + 128, half * 128 : half * 128 + 128
                        ]


def lower_body(gsf, wl, gather_z, mask, low, d4):
    def apart(t, carry):
        i, y = t // 10, t % 10
        pieces = mm(lanes([gsf[i, y], gsf[i + 4, y]]), gather_z[...]).astype(BF)
        for kz in range(4):
            d4[i, y, kz * 64 : kz * 64 + 64, :] = pieces[:, kz * 128 : kz * 128 + 128]
        return carry

    lax.fori_loop(0, 60, apart, 0)
    inside = lanes([mask[0:1, :]] * 2) > 0.5

    def lower(t, carry):
        ix, iy = t // 2, (t % 2) * 2
        window = lanes(
            [
                d4[pl.ds(2 * ix, 4), pl.ds(2 * (iy + e), 4)].reshape(4096, 128)
                for e in range(2)
            ]
        )
        grad = jnp.where(inside, mm(wl[...], window), 0.0).astype(BF)
        for e in range(2):
            low[ix, iy + e] = grad[:, e * 128 : e * 128 + 128]
        return carry

    lax.fori_loop(0, 4, lower, 0)


def sum_body(gup, gconv, out, mine, got0, got1, got2, acc1, acc2, send, recv):
    gx, gy = lax.axis_index("gx"), lax.axis_index("gy")
    core, zlo, x = lax.rem(gx, 2), lax.rem(gx // 2, 2), gx // 4
    zhi, y = lax.rem(gy, 2), gy // 2
    z = zhi * 2 + zlo

    def device(px, py, pz, pc):
        return px * 4 + lax.rem(pz, 2) * 2 + pc, py * 2 + pz // 2

    first = jnp.where(core == 0, x, y)
    second = jnp.where(core == 0, y, x)

    def along_first(step):
        other = lax.rem(first + step, 4)
        return other, device(
            jnp.where(core == 0, other, x), jnp.where(core == 0, y, other), z, core
        )

    def in_plane(step):
        a, b = lax.rem(second + step // 4, 4), lax.rem(z + step % 4, 4)
        return a * 4 + b, device(
            jnp.where(core == 0, x, a), jnp.where(core == 0, a, y), b, core
        )

    twin = device(x, y, z, 1 - core)
    place = second * 4 + z
    barrier = pltpu.get_barrier_semaphore()
    pl.semaphore_signal(barrier, inc=1, device_id=twin, device_id_type=MESH)
    for step in range(1, 4):
        pl.semaphore_signal(barrier, inc=1, device_id=along_first(step)[1], device_id_type=MESH)
    for step in range(1, 16):
        pl.semaphore_signal(barrier, inc=1, device_id=in_plane(step)[1], device_id_type=MESH)

    mine[0:U_ROWS] = gup[...]
    mine[U_ROWS : U_ROWS + 2 * C_ROWS] = gconv[...]
    mine[U_ROWS + 2 * C_ROWS : ROWS] = jnp.zeros((ROWS - U_ROWS - 2 * C_ROWS, 128), BF)
    pl.semaphore_wait(barrier, 19)

    half, quarter, chunk = ROWS // 2, ROWS // 8, ROWS // 128

    def remote(src, dst, at, to):
        return pltpu.make_async_remote_copy(
            src_ref=src,
            dst_ref=dst,
            send_sem=send.at[at],
            recv_sem=recv.at[at],
            device_id=to,
            device_id_type=MESH,
        )

    def rows(start, count):
        return pl.ds(pl.multiple_of(start, 16), count)

    copy = remote(mine.at[rows((1 - core) * half, half)], got0, 0, twin)
    copy.start()
    copy.wait()

    def add0(t, carry):
        at = rows(t * 256, 256)
        own = mine[rows(core * half + t * 256, 256)].astype(F32)
        got0[at] = (own + got0[at].astype(F32)).astype(BF)
        return carry

    lax.fori_loop(0, half // 256, add0, 0)

    copies = []
    for step in range(1, 4):
        other, to = along_first(step)
        copies.append(remote(got0.at[rows(other * quarter, quarter)], got1.at[step - 1], step, to))
    for copy in copies:
        copy.start()
    for copy in copies:
        copy.wait()

    def add1(t, carry):
        at = rows(t * 128, 128)
        total = got0[rows(first * quarter + t * 128, 128)].astype(F32)
        for step in range(3):
            total += got1[step, at].astype(F32)
        acc1[at] = total.astype(BF)
        return carry

    lax.fori_loop(0, quarter // 128, add1, 0)

    copies = []
    for step in range(1, 16):
        other, to = in_plane(step)
        copies.append(
            remote(acc1.at[rows(other * chunk, chunk)], got2.at[step - 1], 3 + step, to)
        )
    for copy in copies:
        copy.start()
    for copy in copies:
        copy.wait()
    total = acc1[rows(place * chunk, chunk)].astype(F32)
    for step in range(15):
        total += got2[step].astype(F32)
    acc2[rows(place * chunk, chunk)] = total.astype(BF)

    copies = []
    for step in range(1, 16):
        other, to = in_plane(step)
        own = acc2.at[rows(place * chunk, chunk)]
        copies.append(remote(own, own, 18 + step, to))
    for copy in copies:
        copy.start()
    for copy in copies:
        copy.wait()
    base = core * half + first * quarter
    copies = []
    for step in range(1, 4):
        other, to = along_first(step)
        copies.append(remote(acc2, out.at[rows(base, quarter)], 33 + step, to))
    for copy in copies:
        copy.start()
    out[rows(base, quarter)] = acc2[...]
    for copy in copies:
        copy.wait()
    own = out.at[rows(core * half, half)]
    copy = remote(own, own, 37, twin)
    copy.start()
    copy.wait()


def sum_over_devices(gup, gconv):
    return call(
        sum_body,
        shape((ROWS, 128)),
        [
            pltpu.VMEM((ROWS, 128), BF),
            pltpu.VMEM((ROWS // 2, 128), BF),
            pltpu.VMEM((3, ROWS // 8, 128), BF),
            pltpu.VMEM((15, ROWS // 128, 128), BF),
            pltpu.VMEM((ROWS // 8, 128), BF),
            pltpu.VMEM((ROWS // 8, 128), BF),
            pltpu.SemaphoreType.DMA((38,)),
            pltpu.SemaphoreType.DMA((38,)),
        ],
        5,
    )(gup, gconv)


def spread_matrix():
    row = lax.broadcasted_iota(jnp.int32, (512, 256), 0)
    column = lax.broadcasted_iota(jnp.int32, (512, 256), 1)
    kz, h, j = row // 128, (row // 64) % 2, row % 64
    hit = (h == column // 128) & (column % 128 == 2 * j - 1 + kz)
    return hit.astype(BF)


def widen_matrix():
    row = lax.broadcasted_iota(jnp.int32, (128, 128), 0)
    column = lax.broadcasted_iota(jnp.int32, (128, 128), 1)
    return (row == 64 + column // 2).astype(BF)


def body(coarse, skip, occupancy, cotangent, up_weight, conv_weight, conv_bias):
    active_z = occupancy[0, 0] > 0
    coarse_mask = jnp.repeat(active_z, EDGE // 2)
    fine_mask = jnp.repeat(active_z, EDGE).astype(F32)
    coarse_t = jnp.transpose(coarse, (1, 2, 0, 3))
    coarse_t = jnp.concatenate(
        [
            jnp.where(coarse_mask, coarse_t, jnp.zeros_like(coarse_t)),
            jnp.broadcast_to(coarse_mask.astype(BF), coarse_t.shape),
        ],
        axis=3,
    )
    skip_t = jnp.transpose(skip, (1, 2, 0, 3))
    cot_t = jnp.transpose(cotangent, (1, 2, 0, 3))
    split = jnp.flip(up_weight.reshape(2, 2, 2, 2, 4, 128, 64), (0, 2))
    wu = jnp.transpose(split, (1, 3, 4, 6, 0, 2, 5)).reshape(1024, 512)
    wl = jnp.transpose(up_weight, (3, 0, 1, 2, 4)).reshape(128, 4096)
    wc = jnp.transpose(conv_weight, (2, 4, 0, 1, 3)).reshape(192, 576)
    flipped = jnp.flip(conv_weight, (0, 1, 2))
    wb = jnp.transpose(flipped, (2, 3, 0, 1, 4)).reshape(192, 576)
    bias = jnp.broadcast_to(conv_bias[:, None], (64, 128))
    spread_up = spread_matrix()
    gather_z = spread_up.T
    mask8 = jnp.broadcast_to(fine_mask, (8, 128))
    cmask = coarse_mask.astype(F32)
    cmask8 = jnp.broadcast_to(jnp.concatenate([cmask, cmask]), (8, 128))

    sf, cf = exchange([skip_t, coarse_t], 1)
    feat, gp, ac, gconv = call(
        front_body,
        [
            shape((8, 8, 64, 128)),
            shape((8, 8, 64, 128)),
            shape((4, 6, 128, 128)),
            shape((2 * C_ROWS, 128)),
        ],
        [
            pltpu.VMEM((10, 10, 64, 128), BF),
            pltpu.VMEM((4, 8, 192, 256), BF),
            pltpu.VMEM((3, 3, 16, 128), F32),
            pltpu.VMEM((C_ROWS, 192), F32),
        ],
    )(sf, cf, cot_t, wu, wc, bias, spread_up, widen_matrix())
    (gpf,) = exchange([gp], 2)
    gs, gup = call(
        back_body,
        [shape((8, 8, 64, 128)), shape((U_ROWS, 128))],
        [pltpu.VMEM((4, 8, 256, 128), BF)],
    )(gpf, ac, wb, gather_z, mask8)
    (gsf,) = exchange([gs], 3)
    total = sum_over_devices(gup, gconv)
    low = call(
        lower_body,
        shape((2, 4, 128, 128)),
        [pltpu.VMEM((6, 10, 256, 128), BF)],
    )(gsf, wl, gather_z, cmask8)

    features = jnp.transpose(feat, (2, 0, 1, 3))
    grad_skip = jnp.transpose(gs, (2, 0, 1, 3))
    low = low.reshape(2, 4, 128, 2, 64)
    grad_coarse = jnp.transpose(low, (2, 3, 0, 1, 4)).reshape(128, 4, 4, 64)
    cells = 8192 * lax.axis_size("gx") * lax.axis_size("gy")
    scale = float(cells) ** -0.5
    up = total[:U_ROWS].astype(F32).reshape(4, 4, 2, 128, 2, 64)
    grad_up = jnp.transpose(up, (0, 1, 2, 4, 3, 5)).reshape(4, 4, 4, 128, 64) * scale
    left = total[U_ROWS : U_ROWS + C_ROWS].astype(F32)
    right = total[U_ROWS + C_ROWS : U_ROWS + 2 * C_ROWS].astype(F32)
    left, right = left * scale, right * scale
    taps = jnp.stack([left[:576, 0:64], left[:576, 64:128], right[:576, 0:64]])
    grad_conv = jnp.transpose(taps.reshape(3, 3, 3, 64, 64), (1, 2, 0, 3, 4))
    grad_bias = left[576, 64:128]
    return features, grad_skip, grad_coarse, grad_up, grad_conv, grad_bias


def solution(mesh):
    field = P(None, "gx", "gy", None)
    return jax.shard_map(
        body,
        mesh=mesh,
        in_specs=(field, field, P("gx", "gy", None), field, P(), P(), P()),
        out_specs=(field, field, field, P(), P(), P()),
        check_vma=False,
    )
```

time: 630 us -> 199 us (0.32); the launches traced: 620 us -> 199 us
  matrix products: 289 us -> 0 us
  Pallas kernels: 0 us -> 156 us
  waiting for transfers between devices: 97.2 us -> 0 us
  blocking collectives: 76.3 us -> 0 us
  starting transfers between devices: 50.9 us -> 0 us
  other arithmetic: 34 us -> 7.6 us
  local copies, waits for them, and re-layouts: 57.5 us -> 34.8 us
  between operations: 15.1 us -> 0.86 us
    conv_general_dilated x4 -> x0, matrix products: 198 us -> none  [convolve(): lax.conv_general_dilated(field[None], kernel, strides, [(0, 0)] * 3, lhs_...]
    pallas_call x0 -> x7, Pallas kernels: none -> 156 us  [the longest x3 63.2 us: exchange(): return call(exchange_body, outs, sems, collective)(*blocks)]
    transpose x2 -> x0, matrix products: 91.4 us -> none  [the longest x1 63.5 us: body(): jnp.transpose(kernel_grad(mixed_pad, grad_pre, (1, 1, 1)), (2, 3, 4, 0, 1))]
    psum x1 -> x0, blocking collectives: 76.3 us -> none  [body(): lax.psum((up_part, conv_part, bias_part), ('gx', 'gy'))]
    psum x1 -> x0, waiting for transfers between devices: 61.2 us -> none  [body(): lax.psum((up_part, conv_part, bias_part), ('gx', 'gy'))]
    ppermute x16 -> x0, starting transfers between devices: 50.9 us -> none  [the longest x8 36.8 us: padded_2(): lax.ppermute(tail, axis, [(i, (i + 1) % count) for i in range(ends)])]
    ppermute x16 -> x0, waiting for transfers between devices: 36 us -> none  [the longest x8 18.4 us: padded_2(): lax.ppermute(head, axis, [((i + 1) % count, i) for i in range(ends)])]
    conv_general_dilated x15 -> x0, local copies, waits for them, and re-layouts: 32.5 us -> none  [convolve(): lax.conv_general_dilated(field[None], kernel, strides, [(0, 0)] * 3, lhs_...]
  transfers between devices with their start and end apart: 17 -> 0, of which waited for: 10 -> 0; matrix products, arithmetic and copies ran while one was open for 16% -> 0% of each run, Pallas kernels for 0% -> 0%
where the time goes in v1:
time: 199 us
  Pallas kernels  156 us (78%)
  local copies, waits for them, and re-layouts  34.8 us (17%)
  other arithmetic  7.6 us (4%)
    pallas_call x3, Pallas kernels, exchange(): return call(exchange_body, outs, sems, collective)(*blocks)  63.2 us
    pallas_call x1, Pallas kernels, sum_over_devices(): call(sum_body, shape((ROWS, 128)), [pltpu.VMEM((ROWS, 128), BF), pltpu.VM...  38.4 us
    pallas_call x1, Pallas kernels, body(): call(front_body, [shape((8, 8, 64, 128)), shape((8, 8, 64, 128)), shape((...  26.6 us
    pallas_call x1, Pallas kernels, body(): call(lower_body, shape((2, 4, 128, 128)), [pltpu.VMEM((6, 10, 256, 128),...  14.5 us
    pallas_call x1, Pallas kernels, body(): call(back_body, [shape((8, 8, 64, 128)), shape((U_ROWS, 128))], [pltpu.VM...  13 us
    unnamed x19, local copies, waits for them, and re-layouts  9.09 us
    mul x3, local copies, waits for them, and re-layouts, body(): jnp.transpose(up, (0, 1, 2, 4, 3, 5)).reshape(4, 4, 4, 128, 64) * scale  7.38 us
    rev x1, local copies, waits for them, and re-layouts, body(): split = jnp.flip(up_weight.reshape(2, 2, 2, 2, 4, 128, 64), (0, 2))  5.46 us

profile of v1, /device:TPU:1, one launch (start us, length us, event | category | flops | bytes accessed | tf_op | source)
XLA Modules:
  0.0 199.0 jit_solution(10889290114126548673)
XLA Ops:
  0.6 0.0 copy-start.4
  0.7 2.0 %fusion.7.spread_up = bf16[512,256]{1,0:T(8,128)(2,1)} fusion(s32[512]{0:T(512)S(1)} %get-tuple-element.44, s32[512]{0:T(512)S(1)} %get-tuple-element.54, s32[512]{0:T(512)S(1)} %get-tuple-element.46, s32[512]{0:T(512)S(1)} %get-tuple-element.47, s32[256]{0:T(256)S(1)} %get-tuple-element.49, s32[256]{0:T(256)S(1)} %get-tuple-element.56, ...), kind=kLoop, calls=%fused_computation.25 | loop fusion | flops 3014656 | bytes 280576 | tf_op jit(solution)/shard_map/convert_element_type | solution.py:500
  2.7 0.7 fusion.19
  3.4 0.1 broadcast_in_dim.28
  3.5 0.1 reshape.54
  3.6 1.2 copy.42
  4.9 0.1 pad.6.clone
  4.9 1.0 pad_maximum_fusion.refs_1_
  5.9 0.0 copy-done.4
  5.9 0.0 copy-start.1
  5.9 1.6 copy.60
  7.5 30.0 %shard_map.118 = (bf16[10,10,64,128]{3,2,1,0:T(8,128)(2,1)}, bf16[6,6,128,128]{3,2,1,0:T(8,128)(2,1)}) custom-call(bf16[8,8,64,128]{3,2,1,0:T(8,128)(2,1)} %bitcast.46, bf16[4,4,128,128]{3,2,1,0:T(8,128)(2,1)} %pad_maximum_fusion.refs_1_), custom_call_target="tpu_custom_call" | custom-call | tf_op jit(solution)/shard_map/pallas_call | solution.py:143
  37.6 0.6 fusion.8.widen
  38.2 0.0 copy-done.1
  38.2 1.1 copy.44
  39.3 5.5 %rev.8 = bf16[2,2,2,2,4,128,64]{5,2,0,6,4,3,1:T(2,128)(2,1)S(1)} reverse(bf16[2,2,2,2,4,128,64]{5,2,0,6,4,3,1:T(2,128)(2,1)S(1)} %copy.44), dimensions={0,2} | reverse | bytes 2097152 | tf_op jit(solution)/shard_map/jit(_flip)/rev | solution.py:523
  44.8 0.0 copy-start.3
  44.8 1.2 reshape.56.wu
  46.0 0.0 copy-start.6
  46.0 2.9 %copy.59 = bf16[64,8,8,128]{3,0,2,1:T(8,128)(2,1)} copy(bf16[64,8,8,128]{3,2,1,0:T(8,128)(2,1)} %param.10) | data formatting | bytes 2097152 | tf_op args[3]
  48.9 0.0 copy-done.3
  48.9 0.8 copy.45
  49.7 1.1 reshape.57.wc
  50.8 0.0 copy-done.6
  50.8 0.7 broadcast_in_dim.32.bias
  51.5 26.6 %shard_map.119 = (bf16[8,8,64,128]{3,2,1,0:T(8,128)(2,1)}, bf16[8,8,64,128]{3,2,1,0:T(8,128)(2,1)}, bf16[4,6,128,128]{3,2,1,0:T(8,128)(2,1)}, bf16[1184,128]{1,0:T(8,128)(2,1)}) custom-call(bf16[10,10,64,128]{3,2,1,0:T(8,128)(2,1)} %get-tuple-element.14.sf, bf16[6,6,128,128]{3,2,1,0:T(8,128)(2,1)} %get-tuple-element.15.cf, bf16[8,8,64,128]{3,2,1,0:T(8,128)(2,1)} %bitcast.49, ...), custom_call_target="tpu_custom_call" | custom-call | tf_op jit(solution)/shard_map/pallas_call | solution.py:537
  78.1 17.5 %shard_map.120.gpf = bf16[10,10,64,128]{3,2,1,0:T(8,128)(2,1)} custom-call(bf16[8,8,64,128]{3,2,1,0:T(8,128)(2,1)} %get-tuple-element.17.refs_0_), custom_call_target="tpu_custom_call" | custom-call | tf_op jit(solution)/shard_map/pallas_call | solution.py:143
  95.6 1.0 fusion.6.gather_z
  96.6 0.1 broadcast_in_dim.33
  96.7 0.1 convert_element_type.35
  96.8 0.6 broadcast_in_dim.34.mask
  97.4 0.4 copy.46
  97.8 1.1 reshape.58.wb
  98.9 13.0 %shard_map.121 = (bf16[8,8,64,128]{3,2,1,0:T(8,128)(2,1)}, bf16[4096,128]{1,0:T(8,128)(2,1)}) custom-call(bf16[10,10,64,128]{3,2,1,0:T(8,128)(2,1)} %shard_map.120.gpf, bf16[4,6,128,128]{3,2,1,0:T(8,128)(2,1)} %get-tuple-element.18.ac, bf16[192,576]{1,0:T(8,128)(2,1)} %reshape.58.wb, bf16[256,512]{1,0:T(8,128)(2,1)} %fusion.6.gather_z, ...), custom_call_target="tpu_custom_call" | custom-call | tf_op jit(solution)/shard_map/pallas_call | solution.py:553
  111.9 38.4 %shard_map.124 = bf16[6144,128]{1,0:T(8,128)(2,1)} custom-call(bf16[4096,128]{1,0:T(8,128)(2,1)} %get-tuple-element.20.gup, bf16[1184,128]{1,0:T(8,128)(2,1)} %get-tuple-element.21.gconv), custom_call_target="tpu_custom_call" | custom-call | tf_op jit(solution)/shard_map/pallas_call | solution.py:478
  150.4 0.0 copy-start
  150.4 1.1 convert_multiply_fusion.1
  151.4 0.1 fusion.20
  151.6 0.9 slice.25
  152.5 1.0 maximum_bitcast_fusion
  153.5 0.0 copy-done
  153.5 0.1 convert_multiply_fusion
  153.7 1.8 copy.50
  155.5 3.0 %mul.34 = f32[4,4,2,128,2,64]{3,2,1,0,5,4:T(2,128)S(1)} reshape(f32[4096,128]{0,1:T(8,128)} %copy.50) | data formatting | bytes 4194304 | tf_op jit(solution)/shard_map/mul | solution.py:573
  158.5 2.5 %copy.51 = f32[4,4,2,2,128,64]{4,5,3,2,1,0:T(8,128)} copy(f32[4,4,2,2,128,64]{4,2,1,0,5,3:T(2,128)S(1)} %bitcast.43) | data formatting | bytes 4194304 | tf_op jit(solution)/shard_map/mul | solution.py:573
  161.1 0.6 slice_bitcast_fusion
  161.6 15.6 %shard_map.122.gsf = bf16[10,10,64,128]{3,2,1,0:T(8,128)(2,1)} custom-call(bf16[8,8,64,128]{3,2,1,0:T(8,128)(2,1)} %get-tuple-element.19.refs_0_), custom_call_target="tpu_custom_call" | custom-call | tf_op jit(solution)/shard_map/pallas_call | solution.py:143
  177.3 0.1 add_convert_fusion
  177.4 0.6 broadcast_in_dim.35.mask
  178.0 1.3 copy.47.wl
  179.3 0.0 copy-start.2
  179.3 14.5 %shard_map.123 = bf16[2,4,128,128]{3,2,1,0:T(8,128)(2,1)} custom-call(bf16[10,10,64,128]{3,2,1,0:T(8,128)(2,1)} %shard_map.122.gsf, bf16[128,4096]{1,0:T(8,128)(2,1)} %copy.47.wl, bf16[256,512]{1,0:T(8,128)(2,1)} %fusion.6.gather_z, f32[8,128]{1,0:T(8,128)} %broadcast_in_dim.35.mask), custom_call_target="tpu_custom_call" | custom-call | tf_op jit(solution)/shard_map/pallas_call | solution.py:560
  193.7 0.0 copy-start.5
  193.7 1.2 copy.48
  195.0 0.7 copy.49
  195.7 0.0 copy-done.2
  195.7 1.6 copy.56
  197.3 0.0 copy-done.5
  197.3 1.6 copy.55
  (14 shorter events, 0.2 us)
Async XLA Ops:
  0.6 5.3 %copy-start.4 = (bf16[64,8,8,128]{3,2,1,0:T(8,128)(2,1)S(1)}, bf16[64,8,8,128]{3,2,1,0:T(8,128)(2,1)}, u32[]{:S(2)}) copy-start(bf16[64,8,8,128]{3,2,1,0:T(8,128)(2,1)} %param.8) | copy-start | bytes 3145732
  5.9 32.3 %copy-start.1 = (bf16[4,4,4,128,64]{3,4,2,1,0:T(8,128)(2,1)S(1)}, bf16[4,4,4,128,64]{3,4,2,1,0:T(8,128)(2,1)}, u32[]{:S(2)}) copy-start(bf16[4,4,4,128,64]{3,4,2,1,0:T(8,128)(2,1)} %param.11) | copy-start | bytes 3145732
  44.8 4.1 %copy-start.3 = (bf16[3,3,3,64,64]{4,3,2,1,0:T(8,128)(2,1)S(1)}, bf16[3,3,3,64,64]{4,3,2,1,0:T(8,128)(2,1)}, u32[]{:S(2)}) copy-start(bf16[3,3,3,64,64]{4,3,2,1,0:T(8,128)(2,1)} %param.12) | copy-start | bytes 663556
  46.0 4.8 %copy-start.6 = (f32[64]{0:T(128)S(1)}, f32[64]{0:T(128)}, u32[]{:S(2)}) copy-start(f32[64]{0:T(128)} %param.13) | copy-start | bytes 772
  150.4 3.2 %copy-start = (bf16[6144,128]{1,0:T(8,128)(2,1)S(1)}, bf16[6144,128]{1,0:T(8,128)(2,1)}, u32[]{:S(2)}) copy-start(bf16[6144,128]{1,0:T(8,128)(2,1)} %shard_map.124) | copy-start | bytes 4718596
  179.3 16.4 %copy-start.2 = (bf16[8,8,64,128]{3,2,1,0:T(8,128)(2,1)S(1)}, bf16[8,8,64,128]{3,2,1,0:T(8,128)(2,1)}, u32[]{:S(2)}) copy-start(bf16[8,8,64,128]{3,2,1,0:T(8,128)(2,1)} %get-tuple-element.19.refs_0_) | copy-start | bytes 3145732
  193.7 3.6 %copy-start.5 = (bf16[8,8,64,128]{3,2,1,0:T(8,128)(2,1)S(1)}, bf16[8,8,64,128]{3,2,1,0:T(8,128)(2,1)}, u32[]{:S(2)}) copy-start(bf16[8,8,64,128]{3,2,1,0:T(8,128)(2,1)} %get-tuple-element.16) | copy-start | bytes 3145732

commit v2 on v0

v2 whole, which is shorter than its diff:
```python
import jax
import jax.numpy as jnp
import ml_dtypes
import numpy as np
from jax import lax
from jax.experimental import pallas as pl
from jax.experimental.pallas import tpu as pltpu
from jax.sharding import PartitionSpec as P

BF = jnp.bfloat16
F32 = jnp.float32
EDGE = 8
MESH = pl.DeviceIdType.MESH
LIMIT = 56 * 2**20

C_ROWS = 592
PIECE = 2048
HALF, QUARTER, CHUNK = PIECE // 2, PIECE // 8, PIECE // 128


def mm(a, b):
    return lax.dot_general(a, b, (((1,), (0,)), ((), ())), preferred_element_type=F32)


def mm_t(a, b):
    return lax.dot_general(a, b, (((1,), (1,)), ((), ())), preferred_element_type=F32)


def lanes(parts):
    return jnp.concatenate(parts, axis=1)


def rows(parts):
    return jnp.concatenate(parts, axis=0)


def shape(dims, kind=BF):
    return jax.ShapeDtypeStruct(dims, kind)


AROUND = [(0, 1), (0, -1), (1, 0), (-1, 0), (1, 1), (1, -1), (-1, 1), (-1, -1)]


def neighbour(dx, dy):
    nx, ny = lax.axis_size("gx"), lax.axis_size("gy")
    gx, gy = lax.axis_index("gx"), lax.axis_index("gy")
    return lax.rem(gx + (dx + nx), nx), lax.rem(gy + (dy + ny), ny)


def outer(step, count):
    if step == 0:
        return pl.ds(1, count), pl.ds(1, count)
    if step > 0:
        return pl.ds(count, 1), pl.ds(0, 1)
    return pl.ds(1, 1), pl.ds(count + 1, 1)


def padding(step, count):
    if step == 0:
        return pl.ds(1, count), pl.ds(1, count)
    if step > 0:
        return pl.ds(count + 1, 1), pl.ds(0, 1)
    return pl.ds(0, 1), pl.ds(count + 1, 1)


def halo_copies(source, target, send, recv, first, place=outer):
    across, along = source.shape[0] - 2, source.shape[1] - 2
    copies = []
    for at, (dx, dy) in enumerate(AROUND):
        sx, tx = place(dx, across)
        sy, ty = place(dy, along)
        copies.append(
            pltpu.make_async_remote_copy(
                src_ref=source.at[sx, sy],
                dst_ref=target.at[tx, ty],
                send_sem=send.at[first + at],
                recv_sem=recv.at[first + at],
                device_id=neighbour(dx, dy),
                device_id_type=MESH,
            )
        )
    return copies


def start(copies):
    for copy in copies:
        copy.start()


def finish(copies):
    for copy in copies:
        copy.wait()


def clear_outside(field):
    across, along = field.shape[0], field.shape[1]
    nx, ny = lax.axis_size("gx"), lax.axis_size("gy")
    gx, gy = lax.axis_index("gx"), lax.axis_index("gy")
    row = jnp.zeros((1,) + field.shape[1:], field.dtype)
    column = jnp.zeros((across, 1) + field.shape[2:], field.dtype)

    @pl.when(gx == 0)
    def _():
        field[0:1] = row

    @pl.when(gx == nx - 1)
    def _():
        field[across - 1 : across] = row

    @pl.when(gy == 0)
    def _():
        field[:, 0:1] = column

    @pl.when(gy == ny - 1)
    def _():
        field[:, along - 1 : along] = column


class Ring:
    def __init__(self):
        gx, gy = lax.axis_index("gx"), lax.axis_index("gy")
        self.core = lax.rem(gx, 2)
        self.x, self.y = gx // 4, gy // 2
        self.z = lax.rem(gy, 2) * 2 + lax.rem(gx // 2, 2)
        self.first = jnp.where(self.core == 0, self.x, self.y)
        self.second = jnp.where(self.core == 0, self.y, self.x)
        self.place = self.second * 4 + self.z
        self.twin = self.device(self.x, self.y, self.z, 1 - self.core)

    def device(self, x, y, z, core):
        return x * 4 + lax.rem(z, 2) * 2 + core, y * 2 + z // 2

    def along_first(self, step):
        other = lax.rem(self.first + step, 4)
        x = jnp.where(self.core == 0, other, self.x)
        y = jnp.where(self.core == 0, self.y, other)
        return other, self.device(x, y, self.z, self.core)

    def in_plane(self, step):
        a, b = lax.rem(self.second + step // 4, 4), lax.rem(self.z + step % 4, 4)
        x = jnp.where(self.core == 0, self.x, a)
        y = jnp.where(self.core == 0, a, self.y)
        return a * 4 + b, self.device(x, y, b, self.core)

    def greet(self, barrier):
        partners = [self.twin]
        partners += [self.along_first(step)[1] for step in range(1, 4)]
        partners += [self.in_plane(step)[1] for step in range(1, 16)]
        for partner in partners:
            pl.semaphore_signal(barrier, inc=1, device_id=partner, device_id_type=MESH)
        return len(partners)


def span(begin, count):
    return pl.ds(pl.multiple_of(begin, 16), count)


class Piece:
    def __init__(self, ring, index, mine, got0, got1, got2, acc1, acc2, out, send, recv):
        self.ring, self.base = ring, index * 38
        self.mine, self.got0, self.got1 = mine.at[index], got0.at[index], got1.at[index]
        self.got2, self.acc1, self.acc2 = got2.at[index], acc1.at[index], acc2.at[index]
        self.out, self.send, self.recv = out.at[index], send, recv
        self.flying = []

    def remote(self, src, dst, at, to):
        return pltpu.make_async_remote_copy(
            src_ref=src,
            dst_ref=dst,
            send_sem=self.send.at[self.base + at],
            recv_sem=self.recv.at[self.base + at],
            device_id=to,
            device_id_type=MESH,
        )

    def launch(self, copies):
        start(copies)
        self.flying = copies

    def step0(self):
        ring = self.ring
        theirs = self.mine.at[span((1 - ring.core) * HALF, HALF)]
        self.launch([self.remote(theirs, self.got0, 0, ring.twin)])

    def step1(self):
        ring = self.ring
        finish(self.flying)

        def add(t, carry):
            own = self.mine[span(ring.core * HALF + t * 256, 256)].astype(F32)
            at = span(t * 256, 256)
            self.got0[at] = (own + self.got0[at].astype(F32)).astype(BF)
            return carry

        lax.fori_loop(0, HALF // 256, add, 0)
        copies = []
        for step in range(1, 4):
            other, to = ring.along_first(step)
            theirs = self.got0.at[span(other * QUARTER, QUARTER)]
            copies.append(self.remote(theirs, self.got1.at[step - 1], step, to))
        self.launch(copies)

    def step2(self):
        ring = self.ring
        finish(self.flying)
        total = self.got0[span(ring.first * QUARTER, QUARTER)].astype(F32)
        for step in range(3):
            total += self.got1[step].astype(F32)
        self.acc1[...] = total.astype(BF)
        copies = []
        for step in range(1, 16):
            other, to = ring.in_plane(step)
            theirs = self.acc1.at[span(other * CHUNK, CHUNK)]
            copies.append(self.remote(theirs, self.got2.at[step - 1], 3 + step, to))
        self.launch(copies)

    def step3(self):
        ring = self.ring
        finish(self.flying)
        total = self.acc1[span(ring.place * CHUNK, CHUNK)].astype(F32)
        for step in range(15):
            total += self.got2[step].astype(F32)
        own = span(ring.place * CHUNK, CHUNK)
        self.acc2[own] = total.astype(BF)
        copies = []
        for step in range(1, 16):
            other, to = ring.in_plane(step)
            copies.append(self.remote(self.acc2.at[own], self.acc2.at[own], 18 + step, to))
        self.launch(copies)

    def step4(self):
        ring = self.ring
        finish(self.flying)
        own = span(ring.core * HALF + ring.first * QUARTER, QUARTER)
        copies = []
        for step in range(1, 4):
            other, to = ring.along_first(step)
            copies.append(self.remote(self.acc2, self.out.at[own], 33 + step, to))
        self.launch(copies)
        self.out[own] = self.acc2[...]

    def step5(self):
        ring = self.ring
        finish(self.flying)
        own = self.out.at[span(ring.core * HALF, HALF)]
        self.launch([self.remote(own, own, 37, ring.twin)])

    def step6(self):
        finish(self.flying)


def lane_of(dims):
    return lax.broadcasted_iota(jnp.int32, dims, len(dims) - 1)


def conv_window(field, i, y):
    return rows(
        [
            lanes(
                [
                    field[i + 4 * h + k, pl.ds(y + e, 3)].reshape(192, 128)
                    for e in range(2)
                    for h in range(2)
                ]
            )
            for k in range(3)
        ]
    )


def join_taps(taps, lane):
    back = jnp.where(lane == 0, 0.0, pltpu.roll(taps[0:64], 1, 1))
    ahead = jnp.where(lane == 127, 0.0, pltpu.roll(taps[128:192], 127, 1))
    return taps[64:128] + back + ahead


def main_body(
    skip,
    cot,
    coarse,
    upw,
    wc,
    wb,
    bias,
    mask_row,
    coarse_mask,
    spread_up,
    gather_z,
    feat,
    gs,
    low,
    total,
    sf,
    cf,
    mf,
    masks,
    cot_t,
    wu,
    wt,
    ac,
    ups,
    mx,
    gpf,
    g3,
    gacc,
    d4,
    acc,
    part,
    part_in,
    mine,
    got0,
    got1,
    got2,
    acc1,
    acc2,
    halo_send,
    halo_recv,
    sum_send,
    sum_recv,
):
    ring = Ring()
    barrier = pltpu.get_barrier_semaphore()
    for dx, dy in AROUND:
        pl.semaphore_signal(barrier, inc=1, device_id=neighbour(dx, dy), device_id_type=MESH)
    greeted = ring.greet(barrier) + len(AROUND)
    lane = lane_of((64, 128))

    keep = coarse_mask[...] > 0.5

    def fill_coarse(t, carry):
        x, y = t // 4, t % 4
        cf[x + 1, y + 1] = jnp.where(keep, coarse[x, y].astype(F32), 0.0).astype(BF)
        return carry

    lax.fori_loop(0, 16, fill_coarse, 0)
    mf[1, 1] = mask_row[...]
    pl.semaphore_wait(barrier, greeted)
    coarse_copies = halo_copies(cf, cf, halo_send, halo_recv, 0)
    mask_copies = halo_copies(mf, mf, halo_send, halo_recv, 8)
    start(coarse_copies)
    start(mask_copies)

    def fill_skip(x, carry):
        sf[x + 1, pl.ds(1, 8)] = jnp.swapaxes(skip[:, x], 0, 1)
        return carry

    lax.fori_loop(0, 8, fill_skip, 0)
    skip_copies = halo_copies(sf, sf, halo_send, halo_recv, 16)
    start(skip_copies)

    def fill_cot(x, carry):
        cot_t[x] = jnp.swapaxes(cot[:, x], 0, 1)
        return carry

    lax.fori_loop(0, 8, fill_cot, 0)
    for sx in range(2):
        for sy in range(2):
            for tx in range(2):
                for ty in range(2):
                    block = upw[2 + sx - 2 * tx, 2 + sy - 2 * ty].reshape(256, 128)
                    at, col = (sx * 2 + sy) * 256, (tx * 2 + ty) * 128
                    wu[at : at + 256, col : col + 128] = block
                    wt[sy, col : col + 128, sx * 256 : sx * 256 + 256] = block.T
    finish(coarse_copies)
    clear_outside(cf)

    def pair_coarse(t, carry):
        i, y = t // 6, t % 6
        ac[i, y] = rows([cf[i, y], cf[i + 2, y]]).T
        return carry

    lax.fori_loop(0, 24, pair_coarse, 0)

    def join(p, q, taps):
        wide = rows(
            [
                lanes([taps[(s * 4 + kz) * 64 : (s * 4 + kz + 1) * 64] for kz in range(4)])
                for s in range(4)
            ]
        )
        up = mm(wide, spread_up[...])
        for s in range(4):
            for h in range(2):
                ups[2 * p + s // 2 + 4 * h, 2 * q + s % 2] = up[
                    s * 64 : s * 64 + 64, h * 128 : h * 128 + 128
                ]

    def up_pair(t, carry):
        p, q = t // 2, (t % 2) * 2
        window = lanes([ac[pl.ds(p, 2), pl.ds(q + e, 2)].reshape(512, 128) for e in range(2)])
        taps = mm(wu[...], window).astype(BF)
        for e in range(2):
            join(p, q + e, taps[:, e * 128 : e * 128 + 128])
        return carry

    lax.fori_loop(0, 6, up_pair, 0)

    def up_last(p, carry):
        join(p, 4, mm(wu[...], ac[pl.ds(p, 2), pl.ds(4, 2)].reshape(512, 128)).astype(BF))
        return carry

    lax.fori_loop(0, 3, up_last, 0)

    finish(mask_copies)
    clear_outside(mf)
    for bx in range(3):
        for by in range(3):
            masks[bx, by] = mf[bx, by].astype(F32)
    finish(skip_copies)

    def mix(t, carry):
        x, y = t // 10, t % 10
        bx = jnp.where(x == 0, 0, jnp.where(x == 9, 2, 1))
        by = jnp.where(y == 0, 0, jnp.where(y == 9, 2, 1))
        value = ups[x, y] + sf[x, y].astype(F32)
        mx[x, y] = jnp.where(masks[bx, by, 0:1, :] > 0.5, value, 0.0).astype(BF)
        return carry

    lax.fori_loop(0, 100, mix, 0, unroll=2)

    inside = masks[1, 1, 0:1, :] > 0.5

    def conv(i, y):
        taps = mm(wc[...], conv_window(mx, i, y))
        for e in range(2):
            for h in range(2):
                at = (e * 2 + h) * 128
                pre = join_taps(taps[:, at : at + 128], lane) + bias[...]
                sig = 1.0 / (1.0 + jnp.exp(-pre))
                feat[i + 4 * h, y + e] = jnp.where(inside, pre * sig, 0.0).astype(BF)
                slope = sig * (1.0 + pre * (1.0 - sig))
                grad = cot_t[i + 4 * h, y + e].astype(F32) * slope
                grad = jnp.where(inside, grad, 0.0).astype(BF)
                gpf[i + 4 * h + 1, y + e + 1] = grad
                wide = grad.astype(F32)
                before = jnp.where(lane == 127, 0.0, pltpu.roll(wide, 127, 1)).astype(BF)
                after = jnp.where(lane == 0, 0.0, pltpu.roll(wide, 1, 1)).astype(BF)
                g3[i, y + e, :, h * 128 : h * 128 + 128] = rows([before, grad, after])

    def conv_outer(t, carry):
        conv(t // 2, (t % 2) * 6)
        return carry

    def conv_inner(t, carry):
        conv(t // 2, 2 + (t % 2) * 2)
        return carry

    gp_copies = halo_copies(gpf, gpf, halo_send, halo_recv, 24)
    lax.fori_loop(0, 8, conv_outer, 0)
    start(gp_copies[0:2])
    start(gp_copies[4:8])
    lax.fori_loop(0, 8, conv_inner, 0)
    start(gp_copies[2:4])

    gacc[...] = jnp.zeros_like(gacc)

    def kernel_grad(t, carry):
        i, y = t // 2, (t % 2) * 4
        grads = lanes([g3[i, y + j] for j in range(4)])
        for k in range(3):
            cells = lanes(
                [
                    mx[i + 4 * h + k, pl.ds(y + j, 3)].reshape(192, 128)
                    for j in range(4)
                    for h in range(2)
                ]
            )
            gacc[k * 192 : k * 192 + 192, :] += mm_t(cells, grads)
        gacc[576:592, :] += mm_t(jnp.ones((16, 1024), BF), grads)
        return carry

    lax.fori_loop(0, 8, kernel_grad, 0)
    mine[2, 0:592] = gacc[:, 0:128].astype(BF)
    mine[2, 592:1184, 0:64] = gacc[:, 128:192].astype(BF)
    mine[2, 592:1184, 64:128] = jnp.zeros((592, 64), BF)
    mine[2, 1184:PIECE] = jnp.zeros((PIECE - 1184, 128), BF)
    sums = [
        Piece(ring, at, mine, got0, got1, got2, acc1, acc2, total, sum_send, sum_recv)
        for at in range(3)
    ]
    sums[2].step0()

    finish(gp_copies)
    clear_outside(gpf)

    def back(t, carry):
        i, y = t // 4, (t % 4) * 2
        taps = mm(wb[...], conv_window(gpf, i, y))
        for e in range(2):
            both = []
            for h in range(2):
                at = (e * 2 + h) * 128
                grad = join_taps(taps[:, at : at + 128], lane)
                grad = jnp.where(inside, grad, 0.0).astype(BF)
                gs[i + 4 * h, y + e] = grad
                both.append(grad)
            apart = mm(lanes(both), gather_z[...]).astype(BF)
            for kz in range(4):
                d4[i, y + e, kz * 64 : kz * 64 + 64, :] = apart[:, kz * 128 : kz * 128 + 128]
        return carry

    lax.fori_loop(0, 8, back, 0)
    sums[2].step1()
    lax.fori_loop(8, 16, back, 0)
    sums[2].step2()

    def up_grad(sx, sy):
        spots = [(pi, qi) for pi in range(1 - sx, 3 - sx) for qi in range(1 - sy, 5 - sy)]
        grads = lanes([d4[2 * pi - 1 + sx, 2 * qi - 1 + sy] for pi, qi in spots])
        cells = rows(
            [
                lanes([ac[pi + tx, qi + ty] for pi, qi in spots])
                for tx in range(2)
                for ty in range(2)
            ]
        )
        result = mm_t(grads, cells).astype(BF)
        for tx in range(2):
            for ty in range(2):
                at, col = (tx * 4 + 2 + sy - 2 * ty) * 256, (tx * 2 + ty) * 128
                mine[sx, at : at + 256, :] = result[:, col : col + 128]

    up_grad(0, 0)
    up_grad(0, 1)
    sums[0].step0()
    sums[2].step3()
    up_grad(1, 0)
    up_grad(1, 1)
    sums[1].step0()
    sums[0].step1()
    sums[2].step4()

    acc[...] = jnp.zeros_like(acc)

    def lower(sy, across):
        if across == 1:
            weight = wt[sy]
            cells = rows([lanes([d4[1 + sx, 2 * q + 1 - sy] for q in range(4)]) for sx in range(2)])
        else:
            sx, i = (1, 0) if across == 0 else (0, 3)
            weight = wt[sy, :, sx * 256 : sx * 256 + 256]
            cells = lanes([d4[i, 2 * q + 1 - sy] for q in range(4)])
        result = mm(weight, cells)
        for tx in range(2):
            for ty in range(2):
                at = (tx * 2 + ty) * 128
                for q in range(4):
                    acc[across + tx, q + ty + 1 - sy] += result[
                        at : at + 128, q * 128 : q * 128 + 128
                    ]

    lower(0, 0)
    lower(1, 0)
    sums[1].step1()
    sums[0].step2()
    sums[2].step5()
    lower(0, 1)
    sums[1].step2()
    sums[0].step3()
    lower(1, 1)
    sums[1].step3()
    sums[0].step4()
    lower(0, 2)
    lower(1, 2)

    def turned(i, y):
        return acc[i, y].T

    def fold(y, carry):
        cells = [turned(i, y) for i in range(4)]
        left, right = [c[0:64] for c in cells], [c[64:128] for c in cells]
        folded = [
            left[0],
            left[1],
            left[2] + right[0],
            left[3] + right[1],
            right[2],
            right[3],
        ]
        for x in range(6):
            part[x, y] = folded[x].astype(BF)
        return carry

    lax.fori_loop(0, 6, fold, 0)
    part_copies = halo_copies(part, part_in, halo_send, halo_recv, 32, padding)
    start(part_copies)
    sums[1].step4()
    sums[0].step5()
    finish(part_copies)
    clear_outside(part_in)
    for x in range(4):
        for y in range(4):
            across = [x + 1] + [0] * (x == 0) + [5] * (x == 3)
            along = [y + 1] + [0] * (y == 0) + [5] * (y == 3)
            value = part[x + 1, y + 1].astype(F32)
            for px in across:
                for py in along:
                    if (px, py) != (x + 1, y + 1):
                        value += part_in[px, py].astype(F32)
            low[x, y] = jnp.where(keep, value, 0.0).astype(BF)
    sums[1].step5()
    sums[2].step6()
    sums[0].step6()
    sums[1].step6()


def spread_matrix():
    row, column = np.arange(512)[:, None], np.arange(256)[None, :]
    kz, h, j = row // 128, (row // 64) % 2, row % 64
    hit = (h == column // 128) & (column % 128 == 2 * j - 1 + kz)
    return hit.astype(ml_dtypes.bfloat16)


def body(coarse, skip, occupancy, cotangent, up_weight, conv_weight, conv_bias):
    active_z = occupancy[0, 0] > 0
    mask_row = jnp.broadcast_to(jnp.repeat(active_z, EDGE).astype(BF), (16, 128))
    coarse_mask = jnp.repeat(active_z, EDGE // 2).astype(F32)
    coarse_mask = jnp.broadcast_to(coarse_mask[:, None], (64, 128))
    coarse_n = jnp.transpose(coarse, (1, 2, 3, 0))
    upw = jnp.transpose(up_weight, (0, 1, 2, 4, 3))
    wc = jnp.transpose(conv_weight, (2, 4, 0, 1, 3)).reshape(192, 576)
    flipped = jnp.flip(conv_weight, (0, 1, 2))
    wb = jnp.transpose(flipped, (2, 3, 0, 1, 4)).reshape(192, 576)
    bias = jnp.broadcast_to(conv_bias[:, None], (64, 128))
    spread_up = spread_matrix()

    feat, gs, low, total = pl.pallas_call(
        main_body,
        out_shape=[
            shape((8, 8, 64, 128)),
            shape((8, 8, 64, 128)),
            shape((4, 4, 64, 128)),
            shape((3, PIECE, 128)),
        ],
        scratch_shapes=[
            pltpu.VMEM((10, 10, 64, 128), BF),
            pltpu.VMEM((6, 6, 64, 128), BF),
            pltpu.VMEM((3, 3, 16, 128), BF),
            pltpu.VMEM((3, 3, 16, 128), F32),
            pltpu.VMEM((8, 8, 64, 128), BF),
            pltpu.VMEM((1024, 512), BF),
            pltpu.VMEM((2, 512, 512), BF),
            pltpu.VMEM((4, 6, 128, 128), BF),
            pltpu.VMEM((10, 10, 64, 128), F32),
            pltpu.VMEM((10, 10, 64, 128), BF),
            pltpu.VMEM((10, 10, 64, 128), BF),
            pltpu.VMEM((4, 8, 192, 256), BF),
            pltpu.VMEM((C_ROWS, 192), F32),
            pltpu.VMEM((4, 8, 256, 128), BF),
            pltpu.VMEM((4, 6, 128, 128), F32),
            pltpu.VMEM((6, 6, 64, 128), BF),
            pltpu.VMEM((6, 6, 64, 128), BF),
            pltpu.VMEM((3, PIECE, 128), BF),
            pltpu.VMEM((3, HALF, 128), BF),
            pltpu.VMEM((3, 3, QUARTER, 128), BF),
            pltpu.VMEM((3, 15, CHUNK, 128), BF),
            pltpu.VMEM((3, QUARTER, 128), BF),
            pltpu.VMEM((3, QUARTER, 128), BF),
            pltpu.SemaphoreType.DMA((40,)),
            pltpu.SemaphoreType.DMA((40,)),
            pltpu.SemaphoreType.DMA((3 * 38,)),
            pltpu.SemaphoreType.DMA((3 * 38,)),
        ],
        compiler_params=pltpu.CompilerParams(
            vmem_limit_bytes=LIMIT, collective_id=1, has_side_effects=True
        ),
    )(
        skip,
        cotangent,
        coarse_n,
        upw,
        wc,
        wb,
        bias,
        mask_row,
        coarse_mask,
        spread_up,
        np.ascontiguousarray(spread_up.T),
    )

    features = jnp.transpose(feat, (2, 0, 1, 3))
    grad_skip = jnp.transpose(gs, (2, 0, 1, 3))
    grad_coarse = jnp.transpose(low, (3, 0, 1, 2))
    cells = 8192 * lax.axis_size("gx") * lax.axis_size("gy")
    scale = float(cells) ** -0.5
    up = total[0:2].reshape(2, 2, 4, 4, 64, 128)
    up = jnp.stack([up[0, 1], up[1, 1], up[0, 0], up[1, 0]]).astype(F32) * scale
    grad_up = jnp.transpose(up, (0, 1, 2, 4, 3))
    left = total[2, 0:C_ROWS].astype(F32) * scale
    right = total[2, C_ROWS : 2 * C_ROWS].astype(F32) * scale
    taps = jnp.stack([left[:576, 0:64], left[:576, 64:128], right[:576, 0:64]])
    grad_conv = jnp.transpose(taps.reshape(3, 3, 3, 64, 64), (1, 2, 0, 3, 4))
    grad_bias = left[576, 64:128]
    return features, grad_skip, grad_coarse, grad_up, grad_conv, grad_bias


def solution(mesh):
    field = P(None, "gx", "gy", None)
    return jax.shard_map(
        body,
        mesh=mesh,
        in_specs=(field, field, P("gx", "gy", None), field, P(), P(), P()),
        out_specs=(field, field, field, P(), P(), P()),
        check_vma=False,
    )
```

time: 630 us -> 115 us (0.18); the launches traced: 620 us -> 114 us
  matrix products: 289 us -> 0 us
  waiting for transfers between devices: 97.2 us -> 0 us
  Pallas kernels: 0 us -> 96.6 us
  blocking collectives: 76.3 us -> 0 us
  starting transfers between devices: 50.9 us -> 0 us
  local copies, waits for them, and re-layouts: 57.5 us -> 13.7 us
  other arithmetic: 34 us -> 3.32 us
  between operations: 15.1 us -> 0.74 us
    conv_general_dilated x4 -> x0, matrix products: 198 us -> none  [convolve(): lax.conv_general_dilated(field[None], kernel, strides, [(0, 0)] * 3, lhs_...]
    pallas_call x0 -> x1, Pallas kernels: none -> 96.6 us  [body(): pl.pallas_call(main_body, out_shape=[shape((8, 8, 64, 128)), shape((8, 8,...]
    transpose x2 -> x0, matrix products: 91.4 us -> none  [the longest x1 63.5 us: body(): jnp.transpose(kernel_grad(mixed_pad, grad_pre, (1, 1, 1)), (2, 3, 4, 0, 1))]
    psum x1 -> x0, blocking collectives: 76.3 us -> none  [body(): lax.psum((up_part, conv_part, bias_part), ('gx', 'gy'))]
    psum x1 -> x0, waiting for transfers between devices: 61.2 us -> none  [body(): lax.psum((up_part, conv_part, bias_part), ('gx', 'gy'))]
    ppermute x16 -> x0, starting transfers between devices: 50.9 us -> none  [the longest x8 36.8 us: padded_2(): lax.ppermute(tail, axis, [(i, (i + 1) % count) for i in range(ends)])]
    ppermute x16 -> x0, waiting for transfers between devices: 36 us -> none  [the longest x8 18.4 us: padded_2(): lax.ppermute(head, axis, [((i + 1) % count, i) for i in range(ends)])]
    conv_general_dilated x15 -> x0, local copies, waits for them, and re-layouts: 32.5 us -> none  [convolve(): lax.conv_general_dilated(field[None], kernel, strides, [(0, 0)] * 3, lhs_...]
  transfers between devices with their start and end apart: 17 -> 0, of which waited for: 10 -> 0; matrix products, arithmetic and copies ran while one was open for 16% -> 0% of each run, Pallas kernels for 0% -> 0%
where the time goes in v2:
time: 115 us; the launch traced here: 114 us
  Pallas kernels  96.6 us (84%)
  local copies, waits for them, and re-layouts  13.7 us (12%)
  other arithmetic  3.32 us (3%)
    pallas_call x1, Pallas kernels, body(): pl.pallas_call(main_body, out_shape=[shape((8, 8, 64, 128)), shape((8, 8,...  96.6 us
    unnamed x11, local copies, waits for them, and re-layouts  5.39 us

profile of v2, /device:TPU:1, one launch (start us, length us, event | category | flops | bytes accessed | tf_op | source)
XLA Modules:
  0.0 114.4 jit_solution(17049755437209212365)
XLA Ops:
  0.6 0.0 copy-start
  0.6 0.7 fusion
  1.4 0.1 broadcast_in_dim.22
  1.4 0.1 convert_element_type.35
  1.5 0.6 broadcast_in_dim.23.mask_row
  2.1 0.1 broadcast_in_dim.24
  2.2 0.1 convert_element_type.37
  2.3 0.7 broadcast_in_dim.25.coarse_mask
  3.0 1.3 %broadcast_in_dim.10.bias = f32[64,128]{1,0:T(8,128)} broadcast(f32[64]{0:T(128)} %param.15), dimensions={0} | broadcast | bytes 33024 | tf_op jit(solution)/shard_map/broadcast_in_dim | solution.py:624
  4.3 1.0 reverse_bitcast_fusion
  5.4 0.4 copy.23
  5.8 1.1 reshape.51.wb
  6.9 0.0 copy-done
  6.9 0.8 copy.22
  7.7 1.1 reshape.50.wc
  8.8 96.6 %shard_map.136 = (bf16[8,8,64,128]{3,2,1,0:T(8,128)(2,1)}, bf16[8,8,64,128]{3,2,1,0:T(8,128)(2,1)}, bf16[4,4,64,128]{3,2,1,0:T(8,128)(2,1)}, bf16[3,2048,128]{2,1,0:T(8,128)(2,1)}) custom-call(bf16[64,8,8,128]{3,2,1,0:T(8,128)(2,1)} %skip.1, bf16[64,8,8,128]{3,2,1,0:T(8,128)(2,1)} %cot.1, bf16[4,4,64,128]{3,2,1,0:T(8,128)(2,1)} %bitcast.48, ...), custom_call_target="tpu_custom_call" | custom-call | tf_op jit(solution)/shard_map/pallas_call | solution.py:627
  105.4 0.0 copy-start.2
  105.4 0.0 copy-start.1
  105.4 3.0 %copy.27 = bf16[64,8,8,128]{3,2,1,0:T(8,128)(2,1)} copy(bf16[64,8,8,128]{3,0,2,1:T(8,128)(2,1)} %bitcast.47) | data formatting | bytes 2097152
  108.5 0.0 copy-done.2
  108.5 1.6 %copy.28 = bf16[64,8,8,128]{3,2,1,0:T(8,128)(2,1)} copy(bf16[64,8,8,128]{3,0,2,1:T(8,128)(2,1)S(1)} %bitcast.46) | data formatting | bytes 2097152
  110.1 0.0 copy-done.1
  110.2 0.1 slice.33
  110.3 0.1 slice_bitcast_fusion.3
  110.4 0.6 slice_bitcast_fusion.4
  110.9 0.1 fusion.2
  111.1 0.0 copy-start.3
  111.1 1.0 maximum_bitcast_fusion
  112.1 1.6 %multiply_bitcast_fusion = f32[4,4,4,128,64]{3,4,2,1,0:T(8,128)} fusion(bf16[1,4,4,64,128]{4,3,2,1,0:T(8,128)(2,1)S(1)} %get-tuple-element.29, bf16[1,4,4,64,128]{4,3,2,1,0:T(8,128)(2,1)S(1)} %get-tuple-element.30, bf16[1,4,4,64,128]{4,3,2,1,0:T(8,128)(2,1)S(1)} %get-tuple-element.31, bf16[1,4,4,64,128]{4,3,2,1,0:T(8,128)(2,1)S(1)} %get-tuple-element.28), kind=kLoop, calls=%fused_computation | loop fusion | flops 2621440 | bytes 3145728 | tf_op jit(solution)/shard_map/transpose | solution.py:688
  113.7 0.0 copy-done.3
  113.7 0.7 copy.30
  (2 shorter events, 0.1 us)
Async XLA Ops:
  0.6 6.2 %copy-start = (bf16[3,3,3,64,64]{4,3,2,1,0:T(8,128)(2,1)S(1)}, bf16[3,3,3,64,64]{4,3,2,1,0:T(8,128)(2,1)}, u32[]{:S(2)}) copy-start(bf16[3,3,3,64,64]{4,3,2,1,0:T(8,128)(2,1)} %param.14) | copy-start | bytes 663556
  105.4 3.0 %copy-start.2 = (bf16[8,8,64,128]{3,2,1,0:T(8,128)(2,1)S(1)}, bf16[8,8,64,128]{3,2,1,0:T(8,128)(2,1)}, u32[]{:S(2)}) copy-start(bf16[8,8,64,128]{3,2,1,0:T(8,128)(2,1)} %get-tuple-element.11) | copy-start | bytes 3145732
  105.4 4.7 %copy-start.1 = (bf16[3,2048,128]{2,1,0:T(8,128)(2,1)S(1)}, bf16[3,2048,128]{2,1,0:T(8,128)(2,1)}, u32[]{:S(2)}) copy-start(bf16[3,2048,128]{2,1,0:T(8,128)(2,1)} %get-tuple-element.13) | copy-start | bytes 4718596
  111.1 2.6 %copy-start.3 = (bf16[4,4,64,128]{3,2,1,0:T(8,128)(2,1)S(1)}, bf16[4,4,64,128]{3,2,1,0:T(8,128)(2,1)}, u32[]{:S(2)}) copy-start(bf16[4,4,64,128]{3,2,1,0:T(8,128)(2,1)} %get-tuple-element.12) | copy-start | bytes 786436

commit v3 on v2

--- a/solution.py
+++ b/solution.py
@@ -1,3 +1,5 @@
+import functools
+
 import jax
 import jax.numpy as jnp
 import ml_dtypes
@@ -275,26 +277,38 @@
 
 
 def main_body(
+    skip_any,
+    cot_any,
+    upw_any,
+    coarse,
+    convw,
+    conv_bias,
+    occupancy,
+    spread_up,
+    gather_z,
+    wide_rows,
+    wide_columns,
+    feat_any,
+    gs_any,
+    low,
+    total,
     skip,
     cot,
-    coarse,
     upw,
-    wc,
-    wb,
-    bias,
-    mask_row,
-    coarse_mask,
-    spread_up,
-    gather_z,
     feat,
     gs,
-    low,
-    total,
+    feat_t,
+    gs_t,
+    local_sem,
     sf,
     cf,
     mf,
     masks,
+    keep_ref,
+    bias,
     cot_t,
+    wc,
+    wb,
     wu,
     wt,
     ac,
@@ -323,36 +337,59 @@
     for dx, dy in AROUND:
         pl.semaphore_signal(barrier, inc=1, device_id=neighbour(dx, dy), device_id_type=MESH)
     greeted = ring.greet(barrier) + len(AROUND)
+    loads = [
+        pltpu.make_async_copy(skip_any, skip, local_sem.at[0]),
+        pltpu.make_async_copy(cot_any, cot, local_sem.at[1]),
+        pltpu.make_async_copy(upw_any, upw, local_sem.at[2]),
+    ]
+    start(loads)
     lane = lane_of((64, 128))
 
-    keep = coarse_mask[...] > 0.5
+    there = jnp.where(occupancy[0] > 0, 1.0, 0.0)
+    mf[1, 1] = mm(jnp.broadcast_to(there, (16, 16)).astype(BF), wide_rows[...]).astype(BF)
+    keep_ref[...] = mm_t(wide_columns[...], jnp.broadcast_to(there, (128, 16)).astype(BF))
 
     def fill_coarse(t, carry):
         x, y = t // 4, t % 4
-        cf[x + 1, y + 1] = jnp.where(keep, coarse[x, y].astype(F32), 0.0).astype(BF)
-        return carry
-
-    lax.fori_loop(0, 16, fill_coarse, 0)
-    mf[1, 1] = mask_row[...]
+        own = jnp.where(keep_ref[...] > 0.5, coarse[x, y].astype(F32), 0.0)
+        cf[x + 1, y + 1] = own.astype(BF)
+        return carry
+
+    lax.fori_loop(0, 16, fill_coarse, 0, unroll=4)
     pl.semaphore_wait(barrier, greeted)
     coarse_copies = halo_copies(cf, cf, halo_send, halo_recv, 0)
     mask_copies = halo_copies(mf, mf, halo_send, halo_recv, 8)
     start(coarse_copies)
     start(mask_copies)
 
+    loads[0].wait()
+
     def fill_skip(x, carry):
         sf[x + 1, pl.ds(1, 8)] = jnp.swapaxes(skip[:, x], 0, 1)
         return carry
 
-    lax.fori_loop(0, 8, fill_skip, 0)
+    lax.fori_loop(0, 8, fill_skip, 0, unroll=2)
     skip_copies = halo_copies(sf, sf, halo_send, halo_recv, 16)
     start(skip_copies)
 
+    loads[1].wait()
+
     def fill_cot(x, carry):
         cot_t[x] = jnp.swapaxes(cot[:, x], 0, 1)
         return carry
 
-    lax.fori_loop(0, 8, fill_cot, 0)
+    lax.fori_loop(0, 8, fill_cot, 0, unroll=2)
+    bias[...] = jnp.broadcast_to(conv_bias[...], (128, 64)).T
+    for kz in range(3):
+        for pair in range(5):
+            taps = [(k // 3, k % 3) for k in (2 * pair, 2 * pair + 1) if k < 9]
+            fore = [convw[kx, ky, kz] for kx, ky in taps]
+            aft = [convw[2 - kx, 2 - ky, 2 - kz] for kx, ky in taps]
+            at, col = kz * 64, pair * 128
+            wide = 64 * len(taps)
+            wc[at : at + 64, col : col + wide] = rows(fore).T
+            wb[at : at + 64, col : col + wide] = lanes(aft)
+    loads[2].wait()
     for sx in range(2):
         for sy in range(2):
             for tx in range(2):
@@ -369,7 +406,7 @@
         ac[i, y] = rows([cf[i, y], cf[i + 2, y]]).T
         return carry
 
-    lax.fori_loop(0, 24, pair_coarse, 0)
+    lax.fori_loop(0, 24, pair_coarse, 0, unroll=4)
 
     def join(p, q, taps):
         wide = rows(
@@ -393,13 +430,13 @@
             join(p, q + e, taps[:, e * 128 : e * 128 + 128])
         return carry
 
-    lax.fori_loop(0, 6, up_pair, 0)
+    lax.fori_loop(0, 6, up_pair, 0, unroll=2)
 
     def up_last(p, carry):
         join(p, 4, mm(wu[...], ac[pl.ds(p, 2), pl.ds(4, 2)].reshape(512, 128)).astype(BF))
         return carry
 
-    lax.fori_loop(0, 3, up_last, 0)
+    lax.fori_loop(0, 3, up_last, 0, unroll=3)
 
     finish(mask_copies)
     clear_outside(mf)
@@ -416,7 +453,7 @@
         mx[x, y] = jnp.where(masks[bx, by, 0:1, :] > 0.5, value, 0.0).astype(BF)
         return carry
 
-    lax.fori_loop(0, 100, mix, 0, unroll=2)
+    lax.fori_loop(0, 100, mix, 0, unroll=4)
 
     inside = masks[1, 1, 0:1, :] > 0.5
 
@@ -446,10 +483,10 @@
         return carry
 
     gp_copies = halo_copies(gpf, gpf, halo_send, halo_recv, 24)
-    lax.fori_loop(0, 8, conv_outer, 0)
+    lax.fori_loop(0, 8, conv_outer, 0, unroll=4)
     start(gp_copies[0:2])
     start(gp_copies[4:8])
-    lax.fori_loop(0, 8, conv_inner, 0)
+    lax.fori_loop(0, 8, conv_inner, 0, unroll=4)
     start(gp_copies[2:4])
 
     gacc[...] = jnp.zeros_like(gacc)
@@ -469,7 +506,7 @@
         gacc[576:592, :] += mm_t(jnp.ones((16, 1024), BF), grads)
         return carry
 
-    lax.fori_loop(0, 8, kernel_grad, 0)
+    lax.fori_loop(0, 8, kernel_grad, 0, unroll=4)
     mine[2, 0:592] = gacc[:, 0:128].astype(BF)
     mine[2, 592:1184, 0:64] = gacc[:, 128:192].astype(BF)
     mine[2, 592:1184, 64:128] = jnp.zeros((592, 64), BF)
@@ -499,10 +536,14 @@
                 d4[i, y + e, kz * 64 : kz * 64 + 64, :] = apart[:, kz * 128 : kz * 128 + 128]
         return carry
 
-    lax.fori_loop(0, 8, back, 0)
+    lax.fori_loop(0, 4, back, 0, unroll=4)
     sums[2].step1()
-    lax.fori_loop(8, 16, back, 0)
+    lax.fori_loop(4, 8, back, 0, unroll=4)
     sums[2].step2()
+    lax.fori_loop(8, 12, back, 0, unroll=4)
+    sums[2].step3()
+    lax.fori_loop(12, 16, back, 0, unroll=4)
+    sums[2].step4()
 
     def up_grad(sx, sy):
         spots = [(pi, qi) for pi in range(1 - sx, 3 - sx) for qi in range(1 - sy, 5 - sy)]
@@ -523,12 +564,9 @@
     up_grad(0, 0)
     up_grad(0, 1)
     sums[0].step0()
-    sums[2].step3()
     up_grad(1, 0)
     up_grad(1, 1)
     sums[1].step0()
-    sums[0].step1()
-    sums[2].step4()
 
     acc[...] = jnp.zeros_like(acc)
 
@@ -551,17 +589,13 @@
 
     lower(0, 0)
     lower(1, 0)
-    sums[1].step1()
-    sums[0].step2()
-    sums[2].step5()
     lower(0, 1)
-    sums[1].step2()
-    sums[0].step3()
+    sums[0].step1()
     lower(1, 1)
-    sums[1].step3()
-    sums[0].step4()
     lower(0, 2)
     lower(1, 2)
+    sums[1].step1()
+    sums[2].step5()
 
     def turned(i, y):
         return acc[i, y].T
@@ -584,8 +618,30 @@
     lax.fori_loop(0, 6, fold, 0)
     part_copies = halo_copies(part, part_in, halo_send, halo_recv, 32, padding)
     start(part_copies)
+    sums[0].step2()
+    sums[1].step2()
+
+    def turn_feat(x, carry):
+        feat_t[:, x] = jnp.swapaxes(feat[x], 0, 1)
+        return carry
+
+    lax.fori_loop(0, 8, turn_feat, 0, unroll=2)
+    stores = [
+        pltpu.make_async_copy(feat_t, feat_any, local_sem.at[3]),
+        pltpu.make_async_copy(gs_t, gs_any, local_sem.at[4]),
+    ]
+    start(stores[0:1])
+    sums[0].step3()
+    sums[1].step3()
+
+    def turn_gs(x, carry):
+        gs_t[:, x] = jnp.swapaxes(gs[x], 0, 1)
+        return carry
+
+    lax.fori_loop(0, 8, turn_gs, 0, unroll=2)
+    start(stores[1:2])
+    sums[0].step4()
     sums[1].step4()
-    sums[0].step5()
     finish(part_copies)
     clear_outside(part_in)
     for x in range(4):
@@ -597,11 +653,49 @@
                 for py in along:
                     if (px, py) != (x + 1, y + 1):
                         value += part_in[px, py].astype(F32)
-            low[x, y] = jnp.where(keep, value, 0.0).astype(BF)
+            low[x, y] = jnp.where(keep_ref[...] > 0.5, value, 0.0).astype(BF)
+    sums[0].step5()
     sums[1].step5()
     sums[2].step6()
+    finish(stores)
     sums[0].step6()
     sums[1].step6()
+
+
+def final_body(
+    scale, feat, gs, low, total, features, grad_skip, grad_coarse, up, conv, bias, v0, v1, v2, sem
+):
+    arrive = [
+        pltpu.make_async_copy(feat, v0, sem.at[0]),
+        pltpu.make_async_copy(gs, v1, sem.at[1]),
+        pltpu.make_async_copy(low, v2, sem.at[2]),
+    ]
+    leave = [
+        pltpu.make_async_copy(v0, features, sem.at[3]),
+        pltpu.make_async_copy(v1, grad_skip, sem.at[4]),
+        pltpu.make_async_copy(v2, grad_coarse, sem.at[5]),
+    ]
+    start(arrive)
+    for come, go in zip(arrive, leave):
+        come.wait()
+        go.start()
+    for kx in range(4):
+        sx, tx = kx % 2, 1 - kx // 2
+
+        def column(t, carry):
+            block = total[sx, pl.ds(pl.multiple_of(tx * 1024 + t * 256, 256), 256)]
+            up[kx, t] = (block.astype(F32) * scale).reshape(4, 64, 128)
+            return carry
+
+        lax.fori_loop(0, 4, column, 0)
+    for tap in range(9):
+        left = total[2, tap * 64 : tap * 64 + 64].astype(F32) * scale
+        right = total[2, C_ROWS + tap * 64 : C_ROWS + tap * 64 + 64].astype(F32) * scale
+        conv[tap // 3, tap % 3, 0] = left[:, 0:64]
+        conv[tap // 3, tap % 3, 1] = left[:, 64:128]
+        conv[tap // 3, tap % 3, 2] = right[:, 0:64]
+    bias[...] = (total[2, 576:592].astype(F32) * scale)[0:1, 64:128]
+    finish(leave)
 
 
 def spread_matrix():
@@ -612,32 +706,34 @@
 
 
 def body(coarse, skip, occupancy, cotangent, up_weight, conv_weight, conv_bias):
-    active_z = occupancy[0, 0] > 0
-    mask_row = jnp.broadcast_to(jnp.repeat(active_z, EDGE).astype(BF), (16, 128))
-    coarse_mask = jnp.repeat(active_z, EDGE // 2).astype(F32)
-    coarse_mask = jnp.broadcast_to(coarse_mask[:, None], (64, 128))
-    coarse_n = jnp.transpose(coarse, (1, 2, 3, 0))
-    upw = jnp.transpose(up_weight, (0, 1, 2, 4, 3))
-    wc = jnp.transpose(conv_weight, (2, 4, 0, 1, 3)).reshape(192, 576)
-    flipped = jnp.flip(conv_weight, (0, 1, 2))
-    wb = jnp.transpose(flipped, (2, 3, 0, 1, 4)).reshape(192, 576)
-    bias = jnp.broadcast_to(conv_bias[:, None], (64, 128))
     spread_up = spread_matrix()
-
+    wide_rows = np.repeat(np.eye(16), EDGE, axis=1).astype(ml_dtypes.bfloat16)
+    wide_columns = np.repeat(np.eye(16), EDGE // 2, axis=0).astype(ml_dtypes.bfloat16)
+    vmem, anywhere = pl.BlockSpec(memory_space=pltpu.VMEM), pl.BlockSpec(memory_space=pl.ANY)
+    plane = (64, 8, 8, 128)
     feat, gs, low, total = pl.pallas_call(
         main_body,
-        out_shape=[
-            shape((8, 8, 64, 128)),
-            shape((8, 8, 64, 128)),
-            shape((4, 4, 64, 128)),
-            shape((3, PIECE, 128)),
-        ],
+        out_shape=[shape(plane), shape(plane), shape((4, 4, 64, 128)), shape((3, PIECE, 128))],
+        in_specs=[anywhere] * 3 + [vmem] * 8,
+        out_specs=[anywhere] * 2 + [vmem] * 2,
         scratch_shapes=[
+            pltpu.VMEM(plane, BF),
+            pltpu.VMEM(plane, BF),
+            pltpu.VMEM((4, 4, 4, 64, 128), BF),
+            pltpu.VMEM((8, 8, 64, 128), BF),
+            pltpu.VMEM((8, 8, 64, 128), BF),
+            pltpu.VMEM(plane, BF),
+            pltpu.VMEM(plane, BF),
+            pltpu.SemaphoreType.DMA((5,)),
             pltpu.VMEM((10, 10, 64, 128), BF),
             pltpu.VMEM((6, 6, 64, 128), BF),
             pltpu.VMEM((3, 3, 16, 128), BF),
             pltpu.VMEM((3, 3, 16, 128), F32),
+            pltpu.VMEM((64, 128), F32),
+            pltpu.VMEM((64, 128), F32),
             pltpu.VMEM((8, 8, 64, 128), BF),
+            pltpu.VMEM((192, 576), BF),
+            pltpu.VMEM((192, 576), BF),
             pltpu.VMEM((1024, 512), BF),
             pltpu.VMEM((2, 512, 512), BF),
             pltpu.VMEM((4, 6, 128, 128), BF),
@@ -667,31 +763,40 @@
     )(
         skip,
         cotangent,
-        coarse_n,
-        upw,
-        wc,
-        wb,
-        bias,
-        mask_row,
-        coarse_mask,
+        jnp.transpose(up_weight, (0, 1, 2, 4, 3)),
+        jnp.transpose(coarse, (1, 2, 3, 0)),
+        conv_weight,
+        conv_bias[None],
+        occupancy[0],
         spread_up,
         np.ascontiguousarray(spread_up.T),
+        wide_rows,
+        wide_columns,
     )
-
-    features = jnp.transpose(feat, (2, 0, 1, 3))
-    grad_skip = jnp.transpose(gs, (2, 0, 1, 3))
+    cells = 8192 * lax.axis_size("gx") * lax.axis_size("gy")
+    features, grad_skip, low, up, grad_conv, bias = pl.pallas_call(
+        functools.partial(final_body, float(cells) ** -0.5),
+        out_shape=[
+            shape(plane),
+            shape(plane),
+            shape((4, 4, 64, 128)),
+            shape((4, 4, 4, 64, 128), F32),
+            shape((3, 3, 3, 64, 64), F32),
+            shape((1, 64), F32),
+        ],
+        in_specs=[anywhere] * 3 + [vmem],
+        out_specs=[anywhere] * 3 + [vmem] * 3,
+        scratch_shapes=[
+            pltpu.VMEM(plane, BF),
+            pltpu.VMEM(plane, BF),
+            pltpu.VMEM((4, 4, 64, 128), BF),
+            pltpu.SemaphoreType.DMA((6,)),
+        ],
+        compiler_params=pltpu.CompilerParams(vmem_limit_bytes=LIMIT),
+    )(feat, gs, low, total)
     grad_coarse = jnp.transpose(low, (3, 0, 1, 2))
-    cells = 8192 * lax.axis_size("gx") * lax.axis_size("gy")
-    scale = float(cells) ** -0.5
-    up = total[0:2].reshape(2, 2, 4, 4, 64, 128)
-    up = jnp.stack([up[0, 1], up[1, 1], up[0, 0], up[1, 0]]).astype(F32) * scale
     grad_up = jnp.transpose(up, (0, 1, 2, 4, 3))
-    left = total[2, 0:C_ROWS].astype(F32) * scale
-    right = total[2, C_ROWS : 2 * C_ROWS].astype(F32) * scale
-    taps = jnp.stack([left[:576, 0:64], left[:576, 64:128], right[:576, 0:64]])
-    grad_conv = jnp.transpose(taps.reshape(3, 3, 3, 64, 64), (1, 2, 0, 3, 4))
-    grad_bias = left[576, 64:128]
-    return features, grad_skip, grad_coarse, grad_up, grad_conv, grad_bias
+    return features, grad_skip, grad_coarse, grad_up, grad_conv, bias[0]
 
 
 def solution(mesh):

time: 115 us -> 98.2 us (0.85)
  local copies, waits for them, and re-layouts: 13.7 us -> 0 us
  other arithmetic: 3.32 us -> 0 us
    unnamed x11 -> x0, local copies, waits for them, and re-layouts: 5.39 us -> none
    broadcast_in_dim x5 -> x0, local copies, waits for them, and re-layouts: 2.79 us -> none  [the longest x1 1.34 us: body(): bias = jnp.broadcast_to(conv_bias[:, None], (64, 128))]
    transpose x2 -> x0, other arithmetic: 2.57 us -> none  [the longest x1 1.56 us: body(): grad_up = jnp.transpose(up, (0, 1, 2, 4, 3))]
    transpose x3 -> x0, local copies, waits for them, and re-layouts: 2.23 us -> none  [the longest x2 1.42 us: body(): wb = jnp.transpose(flipped, (2, 3, 0, 1, 4)).reshape(192, 576)]
    reshape x2 -> x0, local copies, waits for them, and re-layouts: 2.2 us -> none  [the longest x1 1.1 us: body(): wb = jnp.transpose(flipped, (2, 3, 0, 1, 4)).reshape(192, 576)]
    pallas_call x1 -> x2, Pallas kernels: 96.6 us -> 97.2 us  [the longest x1 91.5 us: body(): pl.pallas_call(main_body, out_shape=[shape(plane), shape(plane), shape((4...]
where the time goes in v3:
time: 98.2 us; the launch traced here: 98 us
  Pallas kernels  97.2 us (99%)
    pallas_call x1, Pallas kernels, body(): pl.pallas_call(main_body, out_shape=[shape(plane), shape(plane), shape((4...  91.5 us
    pallas_call x1, Pallas kernels, body(): pl.pallas_call(functools.partial(final_body, float(cells) ** (-0.5)), out...  5.69 us

profile of v3, /device:TPU:1, one launch (start us, length us, event | category | flops | bytes accessed | tf_op | source)
XLA Modules:
  0.0 98.0 jit_solution(3348435819011142611)
XLA Ops:
  0.6 91.5 %shard_map.154 = (bf16[64,8,8,128]{3,2,1,0:T(8,128)(2,1)}, bf16[64,8,8,128]{3,2,1,0:T(8,128)(2,1)}, bf16[4,4,64,128]{3,2,1,0:T(8,128)(2,1)}, bf16[3,2048,128]{2,1,0:T(8,128)(2,1)}) custom-call(bf16[64,8,8,128]{3,2,1,0:T(8,128)(2,1)} %skip_any.1, bf16[64,8,8,128]{3,2,1,0:T(8,128)(2,1)} %cot_any.1, bf16[4,4,4,64,128]{4,3,2,1,0:T(8,128)(2,1)} %bitcast.7, ...), custom_call_target="tpu_custom_call" | custom-call | tf_op jit(solution)/shard_map/pallas_call | solution.py:714
  92.1 5.7 %shard_map.155 = (bf16[64,8,8,128]{3,2,1,0:T(8,128)(2,1)}, bf16[64,8,8,128]{3,2,1,0:T(8,128)(2,1)}, bf16[4,4,64,128]{3,2,1,0:T(8,128)(2,1)}, f32[4,4,4,64,128]{4...) custom-call(bf16[64,8,8,128]{3,2,1,0:T(8,128)(2,1)} %get-tuple-element.16.feat, ...), custom_call_target="tpu_custom_call" | custom-call | tf_op jit(solution)/shard_map/pallas_call | solution.py:777

commit v4 on v3

--- a/solution.py
+++ b/solution.py
@@ -16,8 +16,8 @@
 LIMIT = 56 * 2**20
 
 C_ROWS = 592
-PIECE = 2048
-HALF, QUARTER, CHUNK = PIECE // 2, PIECE // 8, PIECE // 128
+SUB = 1024
+HALF, QUARTER, CHUNK = 3 * SUB, 3 * SUB // 4, 3 * SUB // 64
 
 
 def mm(a, b):
@@ -144,9 +144,21 @@
         y = jnp.where(self.core == 0, a, self.y)
         return a * 4 + b, self.device(x, y, b, self.core)
 
+    def across_first(self, step):
+        x = jnp.where(self.core == 0, self.x, lax.rem(self.x + step, 4))
+        y = jnp.where(self.core == 0, lax.rem(self.y + step, 4), self.y)
+        return self.device(x, y, self.z, 1 - self.core)
+
+    def both_cores(self, step):
+        other = lax.rem(self.first + step, 4)
+        x = jnp.where(self.core == 0, other, self.x)
+        y = jnp.where(self.core == 0, self.y, other)
+        return [self.device(x, y, self.z, self.core), self.device(x, y, self.z, 1 - self.core)]
+
     def greet(self, barrier):
         partners = [self.twin]
         partners += [self.along_first(step)[1] for step in range(1, 4)]
+        partners += [self.across_first(step) for step in range(1, 4)]
         partners += [self.in_plane(step)[1] for step in range(1, 16)]
         for partner in partners:
             pl.semaphore_signal(barrier, inc=1, device_id=partner, device_id_type=MESH)
@@ -157,20 +169,19 @@
     return pl.ds(pl.multiple_of(begin, 16), count)
 
 
-class Piece:
-    def __init__(self, ring, index, mine, got0, got1, got2, acc1, acc2, out, send, recv):
-        self.ring, self.base = ring, index * 38
-        self.mine, self.got0, self.got1 = mine.at[index], got0.at[index], got1.at[index]
-        self.got2, self.acc1, self.acc2 = got2.at[index], acc1.at[index], acc2.at[index]
-        self.out, self.send, self.recv = out.at[index], send, recv
+class Sums:
+    def __init__(self, ring, mine, got0, got1, got2, acc1, acc2, out, send, recv):
+        self.ring, self.mine, self.out = ring, mine, out
+        self.got0, self.got1, self.got2, self.acc1, self.acc2 = got0, got1, got2, acc1, acc2
+        self.send, self.recv = send, recv
         self.flying = []
 
     def remote(self, src, dst, at, to):
         return pltpu.make_async_remote_copy(
             src_ref=src,
             dst_ref=dst,
-            send_sem=self.send.at[self.base + at],
-            recv_sem=self.recv.at[self.base + at],
+            send_sem=self.send.at[at],
+            recv_sem=self.recv.at[at],
             device_id=to,
             device_id_type=MESH,
         )
@@ -179,41 +190,50 @@
         start(copies)
         self.flying = copies
 
-    def step0(self):
+    def step0(self, sub):
         ring = self.ring
-        theirs = self.mine.at[span((1 - ring.core) * HALF, HALF)]
-        self.launch([self.remote(theirs, self.got0, 0, ring.twin)])
+        theirs = self.mine.at[1 - ring.core, sub]
+        copy = self.remote(theirs, self.got0.at[pl.ds(sub * SUB, SUB)], sub, ring.twin)
+        copy.start()
+        self.flying = self.flying + [copy]
 
     def step1(self):
         ring = self.ring
         finish(self.flying)
-
-        def add(t, carry):
-            own = self.mine[span(ring.core * HALF + t * 256, 256)].astype(F32)
-            at = span(t * 256, 256)
-            self.got0[at] = (own + self.got0[at].astype(F32)).astype(BF)
-            return carry
-
-        lax.fori_loop(0, HALF // 256, add, 0)
+        for sub in range(3):
+
+            def add(t, carry):
+                own = self.mine[ring.core, sub, span(t * 256, 256)].astype(F32)
+                at = span(sub * SUB + t * 256, 256)
+                self.got0[at] = (own + self.got0[at].astype(F32)).astype(BF)
+                return carry
+
+            lax.fori_loop(0, SUB // 256, add, 0)
         copies = []
         for step in range(1, 4):
             other, to = ring.along_first(step)
             theirs = self.got0.at[span(other * QUARTER, QUARTER)]
-            copies.append(self.remote(theirs, self.got1.at[step - 1], step, to))
+            copies.append(self.remote(theirs, self.got1.at[step - 1], 2 + step, to))
         self.launch(copies)
 
     def step2(self):
         ring = self.ring
         finish(self.flying)
-        total = self.got0[span(ring.first * QUARTER, QUARTER)].astype(F32)
-        for step in range(3):
-            total += self.got1[step].astype(F32)
-        self.acc1[...] = total.astype(BF)
+
+        def add(t, carry):
+            at = span(t * 256, 256)
+            total = self.got0[span(ring.first * QUARTER + t * 256, 256)].astype(F32)
+            for step in range(3):
+                total += self.got1[step, at].astype(F32)
+            self.acc1[at] = total.astype(BF)
+            return carry
+
+        lax.fori_loop(0, QUARTER // 256, add, 0)
         copies = []
         for step in range(1, 16):
             other, to = ring.in_plane(step)
             theirs = self.acc1.at[span(other * CHUNK, CHUNK)]
-            copies.append(self.remote(theirs, self.got2.at[step - 1], 3 + step, to))
+            copies.append(self.remote(theirs, self.got2.at[step - 1], 5 + step, to))
         self.launch(copies)
 
     def step3(self):
@@ -227,7 +247,7 @@
         copies = []
         for step in range(1, 16):
             other, to = ring.in_plane(step)
-            copies.append(self.remote(self.acc2.at[own], self.acc2.at[own], 18 + step, to))
+            copies.append(self.remote(self.acc2.at[own], self.acc2.at[own], 20 + step, to))
         self.launch(copies)
 
     def step4(self):
@@ -236,18 +256,14 @@
         own = span(ring.core * HALF + ring.first * QUARTER, QUARTER)
         copies = []
         for step in range(1, 4):
-            other, to = ring.along_first(step)
-            copies.append(self.remote(self.acc2, self.out.at[own], 33 + step, to))
+            for side, to in enumerate(ring.both_cores(step)):
+                at = 35 + side * 3 + step
+                copies.append(self.remote(self.acc2, self.out.at[own], at, to))
+        copies.append(self.remote(self.acc2, self.out.at[own], 42, ring.twin))
         self.launch(copies)
         self.out[own] = self.acc2[...]
 
     def step5(self):
-        ring = self.ring
-        finish(self.flying)
-        own = self.out.at[span(ring.core * HALF, HALF)]
-        self.launch([self.remote(own, own, 37, ring.twin)])
-
-    def step6(self):
         finish(self.flying)
 
 
@@ -280,12 +296,12 @@
     skip_any,
     cot_any,
     upw_any,
-    coarse,
-    convw,
+    coarse_any,
+    convw_any,
+    spread_any,
+    gather_any,
     conv_bias,
     occupancy,
-    spread_up,
-    gather_z,
     wide_rows,
     wide_columns,
     feat_any,
@@ -295,6 +311,10 @@
     skip,
     cot,
     upw,
+    coarse,
+    convw,
+    spread_up,
+    gather_z,
     feat,
     gs,
     feat_t,
@@ -338,9 +358,13 @@
         pl.semaphore_signal(barrier, inc=1, device_id=neighbour(dx, dy), device_id_type=MESH)
     greeted = ring.greet(barrier) + len(AROUND)
     loads = [
+        pltpu.make_async_copy(coarse_any, coarse, local_sem.at[5]),
         pltpu.make_async_copy(skip_any, skip, local_sem.at[0]),
         pltpu.make_async_copy(cot_any, cot, local_sem.at[1]),
+        pltpu.make_async_copy(convw_any, convw, local_sem.at[6]),
         pltpu.make_async_copy(upw_any, upw, local_sem.at[2]),
+        pltpu.make_async_copy(spread_any, spread_up, local_sem.at[7]),
+        pltpu.make_async_copy(gather_any, gather_z, local_sem.at[8]),
     ]
     start(loads)
     lane = lane_of((64, 128))
@@ -348,6 +372,8 @@
     there = jnp.where(occupancy[0] > 0, 1.0, 0.0)
     mf[1, 1] = mm(jnp.broadcast_to(there, (16, 16)).astype(BF), wide_rows[...]).astype(BF)
     keep_ref[...] = mm_t(wide_columns[...], jnp.broadcast_to(there, (128, 16)).astype(BF))
+
+    loads[0].wait()
 
     def fill_coarse(t, carry):
         x, y = t // 4, t % 4
@@ -362,7 +388,7 @@
     start(coarse_copies)
     start(mask_copies)
 
-    loads[0].wait()
+    loads[1].wait()
 
     def fill_skip(x, carry):
         sf[x + 1, pl.ds(1, 8)] = jnp.swapaxes(skip[:, x], 0, 1)
@@ -372,13 +398,14 @@
     skip_copies = halo_copies(sf, sf, halo_send, halo_recv, 16)
     start(skip_copies)
 
-    loads[1].wait()
+    loads[2].wait()
 
     def fill_cot(x, carry):
         cot_t[x] = jnp.swapaxes(cot[:, x], 0, 1)
         return carry
 
     lax.fori_loop(0, 8, fill_cot, 0, unroll=2)
+    finish(loads[3:7])
     bias[...] = jnp.broadcast_to(conv_bias[...], (128, 64)).T
     for kz in range(3):
         for pair in range(5):
@@ -389,7 +416,6 @@
             wide = 64 * len(taps)
             wc[at : at + 64, col : col + wide] = rows(fore).T
             wb[at : at + 64, col : col + wide] = lanes(aft)
-    loads[2].wait()
     for sx in range(2):
         for sy in range(2):
             for tx in range(2):
@@ -398,15 +424,21 @@
                     at, col = (sx * 2 + sy) * 256, (tx * 2 + ty) * 128
                     wu[at : at + 256, col : col + 128] = block
                     wt[sy, col : col + 128, sx * 256 : sx * 256 + 256] = block.T
-    finish(coarse_copies)
-    clear_outside(cf)
-
-    def pair_coarse(t, carry):
-        i, y = t // 6, t % 6
+
+    def pair_coarse(i, y):
         ac[i, y] = rows([cf[i, y], cf[i + 2, y]]).T
-        return carry
-
-    lax.fori_loop(0, 24, pair_coarse, 0, unroll=4)
+
+    def pair_middle(t, carry):
+        pair_coarse(1 + t // 4, 1 + t % 4)
+        return carry
+
+    def pair_across(t, carry):
+        pair_coarse((t // 6) * 3, t % 6)
+        return carry
+
+    def pair_along(t, carry):
+        pair_coarse(1 + t // 2, (t % 2) * 5)
+        return carry
 
     def join(p, q, taps):
         wide = rows(
@@ -422,38 +454,48 @@
                     s * 64 : s * 64 + 64, h * 128 : h * 128 + 128
                 ]
 
-    def up_pair(t, carry):
-        p, q = t // 2, (t % 2) * 2
-        window = lanes([ac[pl.ds(p, 2), pl.ds(q + e, 2)].reshape(512, 128) for e in range(2)])
+    def upsample(blocks):
+        window = lanes([ac[p : p + 2, q : q + 2].reshape(512, 128) for p, q in blocks])
         taps = mm(wu[...], window).astype(BF)
-        for e in range(2):
-            join(p, q + e, taps[:, e * 128 : e * 128 + 128])
-        return carry
-
-    lax.fori_loop(0, 6, up_pair, 0, unroll=2)
-
-    def up_last(p, carry):
-        join(p, 4, mm(wu[...], ac[pl.ds(p, 2), pl.ds(4, 2)].reshape(512, 128)).astype(BF))
-        return carry
-
-    lax.fori_loop(0, 3, up_last, 0, unroll=3)
+        for at, (p, q) in enumerate(blocks):
+            join(p, q, taps[:, at * 128 : at * 128 + 128])
+
+    lax.fori_loop(0, 8, pair_middle, 0, unroll=4)
+    upsample([(1, 1), (1, 2), (1, 3)])
+    finish(coarse_copies)
+    clear_outside(cf)
+    lax.fori_loop(0, 12, pair_across, 0, unroll=4)
+    lax.fori_loop(0, 4, pair_along, 0, unroll=4)
+    for p in (0, 2):
+        upsample([(p, 0), (p, 1)])
+        upsample([(p, 2), (p, 3)])
+        upsample([(p, 4), (1, p * 2)])
 
     finish(mask_copies)
     clear_outside(mf)
     for bx in range(3):
         for by in range(3):
             masks[bx, by] = mf[bx, by].astype(F32)
-    finish(skip_copies)
-
-    def mix(t, carry):
-        x, y = t // 10, t % 10
+
+    def mix(x, y):
         bx = jnp.where(x == 0, 0, jnp.where(x == 9, 2, 1))
         by = jnp.where(y == 0, 0, jnp.where(y == 9, 2, 1))
         value = ups[x, y] + sf[x, y].astype(F32)
         mx[x, y] = jnp.where(masks[bx, by, 0:1, :] > 0.5, value, 0.0).astype(BF)
-        return carry
-
-    lax.fori_loop(0, 100, mix, 0, unroll=4)
+
+    def mix_middle(t, carry):
+        mix(1 + t // 8, 1 + t % 8)
+        return carry
+
+    def mix_across(t, carry):
+        mix((t // 10) * 9, t % 10)
+        return carry
+
+    def mix_along(t, carry):
+        mix(1 + t // 2, (t % 2) * 9)
+        return carry
+
+    lax.fori_loop(0, 64, mix_middle, 0, unroll=4)
 
     inside = masks[1, 1, 0:1, :] > 0.5
 
@@ -474,19 +516,36 @@
                 after = jnp.where(lane == 0, 0.0, pltpu.roll(wide, 1, 1)).astype(BF)
                 g3[i, y + e, :, h * 128 : h * 128 + 128] = rows([before, grad, after])
 
-    def conv_outer(t, carry):
-        conv(t // 2, (t % 2) * 6)
-        return carry
-
-    def conv_inner(t, carry):
-        conv(t // 2, 2 + (t % 2) * 2)
-        return carry
+    def middle(step):
+        def run(t, carry):
+            step(1 + t // 2, 2 + (t % 2) * 2)
+            return carry
+
+        lax.fori_loop(0, 4, run, 0, unroll=4)
+
+    def ends_along(step):
+        def run(t, carry):
+            step(t // 2, (t % 2) * 6)
+            return carry
+
+        lax.fori_loop(0, 8, run, 0, unroll=4)
+
+    def ends_across(step):
+        def run(t, carry):
+            step((t // 2) * 3, 2 + (t % 2) * 2)
+            return carry
+
+        lax.fori_loop(0, 4, run, 0, unroll=4)
 
     gp_copies = halo_copies(gpf, gpf, halo_send, halo_recv, 24)
-    lax.fori_loop(0, 8, conv_outer, 0, unroll=4)
+    middle(conv)
+    finish(skip_copies)
+    lax.fori_loop(0, 20, mix_across, 0, unroll=4)
+    lax.fori_loop(0, 16, mix_along, 0, unroll=4)
+    ends_along(conv)
     start(gp_copies[0:2])
     start(gp_copies[4:8])
-    lax.fori_loop(0, 8, conv_inner, 0, unroll=4)
+    ends_across(conv)
     start(gp_copies[2:4])
 
     gacc[...] = jnp.zeros_like(gacc)
@@ -507,21 +566,15 @@
         return carry
 
     lax.fori_loop(0, 8, kernel_grad, 0, unroll=4)
-    mine[2, 0:592] = gacc[:, 0:128].astype(BF)
-    mine[2, 592:1184, 0:64] = gacc[:, 128:192].astype(BF)
-    mine[2, 592:1184, 64:128] = jnp.zeros((592, 64), BF)
-    mine[2, 1184:PIECE] = jnp.zeros((PIECE - 1184, 128), BF)
-    sums = [
-        Piece(ring, at, mine, got0, got1, got2, acc1, acc2, total, sum_send, sum_recv)
-        for at in range(3)
-    ]
-    sums[2].step0()
-
-    finish(gp_copies)
-    clear_outside(gpf)
-
-    def back(t, carry):
-        i, y = t // 4, (t % 4) * 2
+    mine[0, 2, 0:C_ROWS] = gacc[:, 0:128].astype(BF)
+    mine[1, 2, 0:C_ROWS, 0:64] = gacc[:, 128:192].astype(BF)
+    mine[1, 2, 0:C_ROWS, 64:128] = jnp.zeros((C_ROWS, 64), BF)
+    for half in range(2):
+        mine[half, 2, C_ROWS:SUB] = jnp.zeros((SUB - C_ROWS, 128), BF)
+    sums = Sums(ring, mine, got0, got1, got2, acc1, acc2, total, sum_send, sum_recv)
+    sums.step0(2)
+
+    def back(i, y):
         taps = mm(wb[...], conv_window(gpf, i, y))
         for e in range(2):
             both = []
@@ -534,16 +587,12 @@
             apart = mm(lanes(both), gather_z[...]).astype(BF)
             for kz in range(4):
                 d4[i, y + e, kz * 64 : kz * 64 + 64, :] = apart[:, kz * 128 : kz * 128 + 128]
-        return carry
-
-    lax.fori_loop(0, 4, back, 0, unroll=4)
-    sums[2].step1()
-    lax.fori_loop(4, 8, back, 0, unroll=4)
-    sums[2].step2()
-    lax.fori_loop(8, 12, back, 0, unroll=4)
-    sums[2].step3()
-    lax.fori_loop(12, 16, back, 0, unroll=4)
-    sums[2].step4()
+
+    middle(back)
+    finish(gp_copies)
+    clear_outside(gpf)
+    ends_along(back)
+    ends_across(back)
 
     def up_grad(sx, sy):
         spots = [(pi, qi) for pi in range(1 - sx, 3 - sx) for qi in range(1 - sy, 5 - sy)]
@@ -558,15 +607,15 @@
         result = mm_t(grads, cells).astype(BF)
         for tx in range(2):
             for ty in range(2):
-                at, col = (tx * 4 + 2 + sy - 2 * ty) * 256, (tx * 2 + ty) * 128
-                mine[sx, at : at + 256, :] = result[:, col : col + 128]
+                at, col = (2 + sy - 2 * ty) * 256, (tx * 2 + ty) * 128
+                mine[tx, sx, at : at + 256] = result[:, col : col + 128]
 
     up_grad(0, 0)
     up_grad(0, 1)
-    sums[0].step0()
+    sums.step0(0)
     up_grad(1, 0)
     up_grad(1, 1)
-    sums[1].step0()
+    sums.step0(1)
 
     acc[...] = jnp.zeros_like(acc)
 
@@ -589,13 +638,11 @@
 
     lower(0, 0)
     lower(1, 0)
+    sums.step1()
     lower(0, 1)
-    sums[0].step1()
     lower(1, 1)
     lower(0, 2)
     lower(1, 2)
-    sums[1].step1()
-    sums[2].step5()
 
     def turned(i, y):
         return acc[i, y].T
@@ -618,8 +665,7 @@
     lax.fori_loop(0, 6, fold, 0)
     part_copies = halo_copies(part, part_in, halo_send, halo_recv, 32, padding)
     start(part_copies)
-    sums[0].step2()
-    sums[1].step2()
+    sums.step2()
 
     def turn_feat(x, carry):
         feat_t[:, x] = jnp.swapaxes(feat[x], 0, 1)
@@ -631,8 +677,7 @@
         pltpu.make_async_copy(gs_t, gs_any, local_sem.at[4]),
     ]
     start(stores[0:1])
-    sums[0].step3()
-    sums[1].step3()
+    sums.step3()
 
     def turn_gs(x, carry):
         gs_t[:, x] = jnp.swapaxes(gs[x], 0, 1)
@@ -640,8 +685,7 @@
 
     lax.fori_loop(0, 8, turn_gs, 0, unroll=2)
     start(stores[1:2])
-    sums[0].step4()
-    sums[1].step4()
+    sums.step4()
     finish(part_copies)
     clear_outside(part_in)
     for x in range(4):
@@ -654,48 +698,65 @@
                     if (px, py) != (x + 1, y + 1):
                         value += part_in[px, py].astype(F32)
             low[x, y] = jnp.where(keep_ref[...] > 0.5, value, 0.0).astype(BF)
-    sums[0].step5()
-    sums[1].step5()
-    sums[2].step6()
     finish(stores)
-    sums[0].step6()
-    sums[1].step6()
+    sums.step5()
 
 
 def final_body(
-    scale, feat, gs, low, total, features, grad_skip, grad_coarse, up, conv, bias, v0, v1, v2, sem
+    scale,
+    feat,
+    gs,
+    low,
+    total,
+    features,
+    grad_skip,
+    grad_coarse,
+    up_any,
+    conv,
+    bias,
+    v0,
+    v1,
+    v2,
+    sums,
+    up,
+    come_sem,
+    go_sem,
 ):
-    arrive = [
-        pltpu.make_async_copy(feat, v0, sem.at[0]),
-        pltpu.make_async_copy(gs, v1, sem.at[1]),
-        pltpu.make_async_copy(low, v2, sem.at[2]),
-    ]
-    leave = [
-        pltpu.make_async_copy(v0, features, sem.at[3]),
-        pltpu.make_async_copy(v1, grad_skip, sem.at[4]),
-        pltpu.make_async_copy(v2, grad_coarse, sem.at[5]),
-    ]
-    start(arrive)
-    for come, go in zip(arrive, leave):
-        come.wait()
-        go.start()
-    for kx in range(4):
-        sx, tx = kx % 2, 1 - kx // 2
-
-        def column(t, carry):
-            block = total[sx, pl.ds(pl.multiple_of(tx * 1024 + t * 256, 256), 256)]
-            up[kx, t] = (block.astype(F32) * scale).reshape(4, 64, 128)
-            return carry
-
-        lax.fori_loop(0, 4, column, 0)
+    def part(at, count):
+        return total.at[pl.ds(at, count)], sums.at[pl.ds(at, count)]
+
+    taps = [(2 + sx - 2 * tx, tx * HALF + sx * SUB) for tx in range(2) for sx in range(2)]
+    pieces = [part(2 * SUB, C_ROWS), part(HALF + 2 * SUB, C_ROWS)]
+    pieces += [part(at, SUB) for kx, at in taps]
+    pieces += [(feat, v0), (gs, v1), (low, v2)]
+    come = [pltpu.make_async_copy(a, b, come_sem.at[n]) for n, (a, b) in enumerate(pieces)]
+    start(come)
+    go = [(v0, features), (v1, grad_skip), (v2, grad_coarse)]
+    go += [(up.at[kx], up_any.at[kx]) for kx, at in taps]
+    go = [pltpu.make_async_copy(a, b, go_sem.at[n]) for n, (a, b) in enumerate(go)]
+    finish(come[0:2])
     for tap in range(9):
-        left = total[2, tap * 64 : tap * 64 + 64].astype(F32) * scale
-        right = total[2, C_ROWS + tap * 64 : C_ROWS + tap * 64 + 64].astype(F32) * scale
+        at = 2 * SUB + tap * 64
+        left = sums[at : at + 64].astype(F32) * scale
+        right = sums[HALF + at : HALF + at + 64].astype(F32) * scale
         conv[tap // 3, tap % 3, 0] = left[:, 0:64]
         conv[tap // 3, tap % 3, 1] = left[:, 64:128]
         conv[tap // 3, tap % 3, 2] = right[:, 0:64]
-    bias[...] = (total[2, 576:592].astype(F32) * scale)[0:1, 64:128]
-    finish(leave)
+    bias[...] = (sums[2 * SUB + 576 : 2 * SUB + 592].astype(F32) * scale)[0:1, 64:128]
+    for n, (kx, at) in enumerate(taps):
+        come[2 + n].wait()
+
+        def column(t, carry):
+            block = sums[pl.ds(pl.multiple_of(at + t * 256, 256), 256)]
+            up[kx, t] = (block.astype(F32) * scale).reshape(4, 64, 128)
+            return carry
+
+        lax.fori_loop(0, 4, column, 0)
+        go[3 + n].start()
+    for n in range(3):
+        come[6 + n].wait()
+        go[n].start()
+    finish(go)
 
 
 def spread_matrix():
@@ -713,18 +774,22 @@
     plane = (64, 8, 8, 128)
     feat, gs, low, total = pl.pallas_call(
         main_body,
-        out_shape=[shape(plane), shape(plane), shape((4, 4, 64, 128)), shape((3, PIECE, 128))],
-        in_specs=[anywhere] * 3 + [vmem] * 8,
+        out_shape=[shape(plane), shape(plane), shape((4, 4, 64, 128)), shape((2 * HALF, 128))],
+        in_specs=[anywhere] * 7 + [vmem] * 4,
         out_specs=[anywhere] * 2 + [vmem] * 2,
         scratch_shapes=[
             pltpu.VMEM(plane, BF),
             pltpu.VMEM(plane, BF),
             pltpu.VMEM((4, 4, 4, 64, 128), BF),
+            pltpu.VMEM((4, 4, 64, 128), BF),
+            pltpu.VMEM((3, 3, 3, 64, 64), BF),
+            pltpu.VMEM((512, 256), BF),
+            pltpu.VMEM((256, 512), BF),
             pltpu.VMEM((8, 8, 64, 128), BF),
             pltpu.VMEM((8, 8, 64, 128), BF),
             pltpu.VMEM(plane, BF),
             pltpu.VMEM(plane, BF),
-            pltpu.SemaphoreType.DMA((5,)),
+            pltpu.SemaphoreType.DMA((9,)),
             pltpu.VMEM((10, 10, 64, 128), BF),
             pltpu.VMEM((6, 6, 64, 128), BF),
             pltpu.VMEM((3, 3, 16, 128), BF),
@@ -746,16 +811,16 @@
             pltpu.VMEM((4, 6, 128, 128), F32),
             pltpu.VMEM((6, 6, 64, 128), BF),
             pltpu.VMEM((6, 6, 64, 128), BF),
-            pltpu.VMEM((3, PIECE, 128), BF),
-            pltpu.VMEM((3, HALF, 128), BF),
-            pltpu.VMEM((3, 3, QUARTER, 128), BF),
-            pltpu.VMEM((3, 15, CHUNK, 128), BF),
+            pltpu.VMEM((2, 3, SUB, 128), BF),
+            pltpu.VMEM((HALF, 128), BF),
             pltpu.VMEM((3, QUARTER, 128), BF),
-            pltpu.VMEM((3, QUARTER, 128), BF),
+            pltpu.VMEM((15, CHUNK, 128), BF),
+            pltpu.VMEM((QUARTER, 128), BF),
+            pltpu.VMEM((QUARTER, 128), BF),
             pltpu.SemaphoreType.DMA((40,)),
             pltpu.SemaphoreType.DMA((40,)),
-            pltpu.SemaphoreType.DMA((3 * 38,)),
-            pltpu.SemaphoreType.DMA((3 * 38,)),
+            pltpu.SemaphoreType.DMA((43,)),
+            pltpu.SemaphoreType.DMA((43,)),
         ],
         compiler_params=pltpu.CompilerParams(
             vmem_limit_bytes=LIMIT, collective_id=1, has_side_effects=True
@@ -766,10 +831,10 @@
         jnp.transpose(up_weight, (0, 1, 2, 4, 3)),
         jnp.transpose(coarse, (1, 2, 3, 0)),
         conv_weight,
+        spread_up,
+        np.ascontiguousarray(spread_up.T),
         conv_bias[None],
         occupancy[0],
-        spread_up,
-        np.ascontiguousarray(spread_up.T),
         wide_rows,
         wide_columns,
     )
@@ -784,13 +849,16 @@
             shape((3, 3, 3, 64, 64), F32),
             shape((1, 64), F32),
         ],
-        in_specs=[anywhere] * 3 + [vmem],
-        out_specs=[anywhere] * 3 + [vmem] * 3,
+        in_specs=[anywhere] * 4,
+        out_specs=[anywhere] * 4 + [vmem] * 2,
         scratch_shapes=[
             pltpu.VMEM(plane, BF),
             pltpu.VMEM(plane, BF),
             pltpu.VMEM((4, 4, 64, 128), BF),
-            pltpu.SemaphoreType.DMA((6,)),
+            pltpu.VMEM((2 * HALF, 128), BF),
+            pltpu.VMEM((4, 4, 4, 64, 128), F32),
+            pltpu.SemaphoreType.DMA((9,)),
+            pltpu.SemaphoreType.DMA((7,)),
         ],
         compiler_params=pltpu.CompilerParams(vmem_limit_bytes=LIMIT),
     )(feat, gs, low, total)

time: 98.2 us -> 90.8 us (0.925)
  Pallas kernels: 97.2 us -> 89.8 us
    pallas_call x1, Pallas kernels: 91.5 us -> 85.5 us  [body(): pl.pallas_call(main_body, out_shape=[shape(plane), shape(plane), shape((4...]
    pallas_call x1, Pallas kernels: 5.69 us -> 4.34 us  [body(): pl.pallas_call(functools.partial(final_body, float(cells) ** (-0.5)), out...]
where the time goes in v4:
time: 90.8 us; the launch traced here: 90.6 us
  Pallas kernels  89.8 us (99%)
    pallas_call x1, Pallas kernels, body(): pl.pallas_call(main_body, out_shape=[shape(plane), shape(plane), shape((4...  85.5 us
    pallas_call x1, Pallas kernels, body(): pl.pallas_call(functools.partial(final_body, float(cells) ** (-0.5)), out...  4.34 us

profile of v4, /device:TPU:1, one launch (start us, length us, event | category | flops | bytes accessed | tf_op | source)
XLA Modules:
  0.0 90.6 jit_solution(8375671000620493254)
XLA Ops:
  0.6 85.5 %shard_map.154 = (bf16[64,8,8,128]{3,2,1,0:T(8,128)(2,1)}, bf16[64,8,8,128]{3,2,1,0:T(8,128)(2,1)}, bf16[4,4,64,128]{3,2,1,0:T(8,128)(2,1)}, bf16[6144,128]{1,0:T(8,128)(2,1)}) custom-call(bf16[64,8,8,128]{3,2,1,0:T(8,128)(2,1)} %skip_any.1, bf16[64,8,8,128]{3,2,1,0:T(8,128)(2,1)} %cot_any.1, bf16[4,4,4,64,128]{4,3,2,1,0:T(8,128)(2,1)} %bitcast.7, ...), custom_call_target="tpu_custom_call" | custom-call | tf_op jit(solution)/shard_map/pallas_call | solution.py:775
  86.1 4.3 %shard_map.155 = (bf16[64,8,8,128]{3,2,1,0:T(8,128)(2,1)}, bf16[64,8,8,128]{3,2,1,0:T(8,128)(2,1)}, bf16[4,4,64,128]{3,2,1,0:T(8,128)(2,1)}, f32[4,4,4,64,128]{4...) custom-call(bf16[64,8,8,128]{3,2,1,0:T(8,128)(2,1)} %get-tuple-element.16.feat, ...), custom_call_target="tpu_custom_call" | custom-call | tf_op jit(solution)/shard_map/pallas_call | solution.py:842

commit v5 on v4

--- a/solution.py
+++ b/solution.py
@@ -16,8 +16,8 @@
 LIMIT = 56 * 2**20
 
 C_ROWS = 592
-SUB = 1024
-HALF, QUARTER, CHUNK = 3 * SUB, 3 * SUB // 4, 3 * SUB // 64
+PIECE = 2048
+HALF, QUARTER, CHUNK = PIECE // 2, PIECE // 8, PIECE // 128
 
 
 def mm(a, b):
@@ -144,21 +144,9 @@
         y = jnp.where(self.core == 0, a, self.y)
         return a * 4 + b, self.device(x, y, b, self.core)
 
-    def across_first(self, step):
-        x = jnp.where(self.core == 0, self.x, lax.rem(self.x + step, 4))
-        y = jnp.where(self.core == 0, lax.rem(self.y + step, 4), self.y)
-        return self.device(x, y, self.z, 1 - self.core)
-
-    def both_cores(self, step):
-        other = lax.rem(self.first + step, 4)
-        x = jnp.where(self.core == 0, other, self.x)
-        y = jnp.where(self.core == 0, self.y, other)
-        return [self.device(x, y, self.z, self.core), self.device(x, y, self.z, 1 - self.core)]
-
     def greet(self, barrier):
         partners = [self.twin]
         partners += [self.along_first(step)[1] for step in range(1, 4)]
-        partners += [self.across_first(step) for step in range(1, 4)]
         partners += [self.in_plane(step)[1] for step in range(1, 16)]
         for partner in partners:
             pl.semaphore_signal(barrier, inc=1, device_id=partner, device_id_type=MESH)
@@ -169,19 +157,20 @@
     return pl.ds(pl.multiple_of(begin, 16), count)
 
 
-class Sums:
-    def __init__(self, ring, mine, got0, got1, got2, acc1, acc2, out, send, recv):
-        self.ring, self.mine, self.out = ring, mine, out
-        self.got0, self.got1, self.got2, self.acc1, self.acc2 = got0, got1, got2, acc1, acc2
-        self.send, self.recv = send, recv
+class Piece:
+    def __init__(self, ring, index, mine, got0, got1, got2, acc1, acc2, out, send, recv):
+        self.ring, self.base = ring, index * 38
+        self.mine, self.got0, self.got1 = mine.at[index], got0.at[index], got1.at[index]
+        self.got2, self.acc1, self.acc2 = got2.at[index], acc1.at[index], acc2.at[index]
+        self.out, self.send, self.recv = out.at[index], send, recv
         self.flying = []
 
     def remote(self, src, dst, at, to):
         return pltpu.make_async_remote_copy(
             src_ref=src,
             dst_ref=dst,
-            send_sem=self.send.at[at],
-            recv_sem=self.recv.at[at],
+            send_sem=self.send.at[self.base + at],
+            recv_sem=self.recv.at[self.base + at],
             device_id=to,
             device_id_type=MESH,
         )
@@ -190,50 +179,41 @@
         start(copies)
         self.flying = copies
 
-    def step0(self, sub):
+    def step0(self):
         ring = self.ring
-        theirs = self.mine.at[1 - ring.core, sub]
-        copy = self.remote(theirs, self.got0.at[pl.ds(sub * SUB, SUB)], sub, ring.twin)
-        copy.start()
-        self.flying = self.flying + [copy]
+        theirs = self.mine.at[span((1 - ring.core) * HALF, HALF)]
+        self.launch([self.remote(theirs, self.got0, 0, ring.twin)])
 
     def step1(self):
         ring = self.ring
         finish(self.flying)
-        for sub in range(3):
-
-            def add(t, carry):
-                own = self.mine[ring.core, sub, span(t * 256, 256)].astype(F32)
-                at = span(sub * SUB + t * 256, 256)
-                self.got0[at] = (own + self.got0[at].astype(F32)).astype(BF)
-                return carry
-
-            lax.fori_loop(0, SUB // 256, add, 0)
+
+        def add(t, carry):
+            own = self.mine[span(ring.core * HALF + t * 256, 256)].astype(F32)
+            at = span(t * 256, 256)
+            self.got0[at] = (own + self.got0[at].astype(F32)).astype(BF)
+            return carry
+
+        lax.fori_loop(0, HALF // 256, add, 0)
         copies = []
         for step in range(1, 4):
             other, to = ring.along_first(step)
             theirs = self.got0.at[span(other * QUARTER, QUARTER)]
-            copies.append(self.remote(theirs, self.got1.at[step - 1], 2 + step, to))
+            copies.append(self.remote(theirs, self.got1.at[step - 1], step, to))
         self.launch(copies)
 
     def step2(self):
         ring = self.ring
         finish(self.flying)
-
-        def add(t, carry):
-            at = span(t * 256, 256)
-            total = self.got0[span(ring.first * QUARTER + t * 256, 256)].astype(F32)
-            for step in range(3):
-                total += self.got1[step, at].astype(F32)
-            self.acc1[at] = total.astype(BF)
-            return carry
-
-        lax.fori_loop(0, QUARTER // 256, add, 0)
+        total = self.got0[span(ring.first * QUARTER, QUARTER)].astype(F32)
+        for step in range(3):
+            total += self.got1[step].astype(F32)
+        self.acc1[...] = total.astype(BF)
         copies = []
         for step in range(1, 16):
             other, to = ring.in_plane(step)
             theirs = self.acc1.at[span(other * CHUNK, CHUNK)]
-            copies.append(self.remote(theirs, self.got2.at[step - 1], 5 + step, to))
+            copies.append(self.remote(theirs, self.got2.at[step - 1], 3 + step, to))
         self.launch(copies)
 
     def step3(self):
@@ -247,7 +227,7 @@
         copies = []
         for step in range(1, 16):
             other, to = ring.in_plane(step)
-            copies.append(self.remote(self.acc2.at[own], self.acc2.at[own], 20 + step, to))
+            copies.append(self.remote(self.acc2.at[own], self.acc2.at[own], 18 + step, to))
         self.launch(copies)
 
     def step4(self):
@@ -256,14 +236,18 @@
         own = span(ring.core * HALF + ring.first * QUARTER, QUARTER)
         copies = []
         for step in range(1, 4):
-            for side, to in enumerate(ring.both_cores(step)):
-                at = 35 + side * 3 + step
-                copies.append(self.remote(self.acc2, self.out.at[own], at, to))
-        copies.append(self.remote(self.acc2, self.out.at[own], 42, ring.twin))
+            other, to = ring.along_first(step)
+            copies.append(self.remote(self.acc2, self.out.at[own], 33 + step, to))
         self.launch(copies)
         self.out[own] = self.acc2[...]
 
     def step5(self):
+        ring = self.ring
+        finish(self.flying)
+        own = self.out.at[span(ring.core * HALF, HALF)]
+        self.launch([self.remote(own, own, 37, ring.twin)])
+
+    def step6(self):
         finish(self.flying)
 
 
@@ -271,13 +255,13 @@
     return lax.broadcasted_iota(jnp.int32, dims, len(dims) - 1)
 
 
-def conv_window(field, i, y):
+def conv_window(field, i, pair):
     return rows(
         [
             lanes(
                 [
-                    field[i + 4 * h + k, pl.ds(y + e, 3)].reshape(192, 128)
-                    for e in range(2)
+                    field[i + 4 * h + k, pl.ds(y, 3)].reshape(192, 128)
+                    for y in pair
                     for h in range(2)
                 ]
             )
@@ -396,7 +380,6 @@
 
     lax.fori_loop(0, 8, fill_skip, 0, unroll=2)
     skip_copies = halo_copies(sf, sf, halo_send, halo_recv, 16)
-    start(skip_copies)
 
     loads[2].wait()
 
@@ -405,6 +388,7 @@
         return carry
 
     lax.fori_loop(0, 8, fill_cot, 0, unroll=2)
+    start(skip_copies)
     finish(loads[3:7])
     bias[...] = jnp.broadcast_to(conv_bias[...], (128, 64)).T
     for kz in range(3):
@@ -499,53 +483,56 @@
 
     inside = masks[1, 1, 0:1, :] > 0.5
 
-    def conv(i, y):
-        taps = mm(wc[...], conv_window(mx, i, y))
-        for e in range(2):
+    def conv(i, pair):
+        taps = mm(wc[...], conv_window(mx, i, pair))
+        for e, y in enumerate(pair):
             for h in range(2):
                 at = (e * 2 + h) * 128
                 pre = join_taps(taps[:, at : at + 128], lane) + bias[...]
                 sig = 1.0 / (1.0 + jnp.exp(-pre))
-                feat[i + 4 * h, y + e] = jnp.where(inside, pre * sig, 0.0).astype(BF)
+                feat[i + 4 * h, y] = jnp.where(inside, pre * sig, 0.0).astype(BF)
                 slope = sig * (1.0 + pre * (1.0 - sig))
-                grad = cot_t[i + 4 * h, y + e].astype(F32) * slope
+                grad = cot_t[i + 4 * h, y].astype(F32) * slope
                 grad = jnp.where(inside, grad, 0.0).astype(BF)
-                gpf[i + 4 * h + 1, y + e + 1] = grad
+                gpf[i + 4 * h + 1, y + 1] = grad
                 wide = grad.astype(F32)
                 before = jnp.where(lane == 127, 0.0, pltpu.roll(wide, 127, 1)).astype(BF)
                 after = jnp.where(lane == 0, 0.0, pltpu.roll(wide, 1, 1)).astype(BF)
-                g3[i, y + e, :, h * 128 : h * 128 + 128] = rows([before, grad, after])
+                g3[i, y, :, h * 128 : h * 128 + 128] = rows([before, grad, after])
 
     def middle(step):
         def run(t, carry):
-            step(1 + t // 2, 2 + (t % 2) * 2)
+            y = 1 + (t % 3) * 2
+            step(1 + t // 3, (y, y + 1))
             return carry
 
-        lax.fori_loop(0, 4, run, 0, unroll=4)
-
-    def ends_along(step):
+        lax.fori_loop(0, 6, run, 0, unroll=3)
+
+    def ends_along(step, first, last):
+        def run(i, carry):
+            step(i, (0, 7))
+            return carry
+
+        lax.fori_loop(first, last, run, 0, unroll=last - first)
+
+    def ends_across(step, i):
         def run(t, carry):
-            step(t // 2, (t % 2) * 6)
+            y = 1 + t * 2
+            step(i, (y, y + 1))
             return carry
 
-        lax.fori_loop(0, 8, run, 0, unroll=4)
-
-    def ends_across(step):
-        def run(t, carry):
-            step((t // 2) * 3, 2 + (t % 2) * 2)
-            return carry
-
-        lax.fori_loop(0, 4, run, 0, unroll=4)
+        lax.fori_loop(0, 3, run, 0, unroll=3)
 
     gp_copies = halo_copies(gpf, gpf, halo_send, halo_recv, 24)
     middle(conv)
     finish(skip_copies)
     lax.fori_loop(0, 20, mix_across, 0, unroll=4)
     lax.fori_loop(0, 16, mix_along, 0, unroll=4)
-    ends_along(conv)
+    ends_along(conv, 0, 4)
     start(gp_copies[0:2])
     start(gp_copies[4:8])
-    ends_across(conv)
+    ends_across(conv, 0)
+    ends_across(conv, 3)
     start(gp_copies[2:4])
 
     gacc[...] = jnp.zeros_like(gacc)
@@ -566,33 +553,30 @@
         return carry
 
     lax.fori_loop(0, 8, kernel_grad, 0, unroll=4)
-    mine[0, 2, 0:C_ROWS] = gacc[:, 0:128].astype(BF)
-    mine[1, 2, 0:C_ROWS, 0:64] = gacc[:, 128:192].astype(BF)
-    mine[1, 2, 0:C_ROWS, 64:128] = jnp.zeros((C_ROWS, 64), BF)
-    for half in range(2):
-        mine[half, 2, C_ROWS:SUB] = jnp.zeros((SUB - C_ROWS, 128), BF)
-    sums = Sums(ring, mine, got0, got1, got2, acc1, acc2, total, sum_send, sum_recv)
-    sums.step0(2)
-
-    def back(i, y):
-        taps = mm(wb[...], conv_window(gpf, i, y))
-        for e in range(2):
+    mine[2, 0:C_ROWS] = gacc[:, 0:128].astype(BF)
+    mine[2, C_ROWS : 2 * C_ROWS, 0:64] = gacc[:, 128:192].astype(BF)
+    mine[2, C_ROWS : 2 * C_ROWS, 64:128] = jnp.zeros((C_ROWS, 64), BF)
+    mine[2, 2 * C_ROWS : PIECE] = jnp.zeros((PIECE - 2 * C_ROWS, 128), BF)
+    sums = [
+        Piece(ring, at, mine, got0, got1, got2, acc1, acc2, total, sum_send, sum_recv)
+        for at in range(3)
+    ]
+    even, odd, conv_sum = sums
+    conv_sum.step0()
+
+    def back(i, pair):
+        taps = mm(wb[...], conv_window(gpf, i, pair))
+        for e, y in enumerate(pair):
             both = []
             for h in range(2):
                 at = (e * 2 + h) * 128
                 grad = join_taps(taps[:, at : at + 128], lane)
                 grad = jnp.where(inside, grad, 0.0).astype(BF)
-                gs[i + 4 * h, y + e] = grad
+                gs[i + 4 * h, y] = grad
                 both.append(grad)
             apart = mm(lanes(both), gather_z[...]).astype(BF)
             for kz in range(4):
-                d4[i, y + e, kz * 64 : kz * 64 + 64, :] = apart[:, kz * 128 : kz * 128 + 128]
-
-    middle(back)
-    finish(gp_copies)
-    clear_outside(gpf)
-    ends_along(back)
-    ends_across(back)
+                d4[i, y, kz * 64 : kz * 64 + 64, :] = apart[:, kz * 128 : kz * 128 + 128]
 
     def up_grad(sx, sy):
         spots = [(pi, qi) for pi in range(1 - sx, 3 - sx) for qi in range(1 - sy, 5 - sy)]
@@ -607,15 +591,27 @@
         result = mm_t(grads, cells).astype(BF)
         for tx in range(2):
             for ty in range(2):
-                at, col = (2 + sy - 2 * ty) * 256, (tx * 2 + ty) * 128
-                mine[tx, sx, at : at + 256] = result[:, col : col + 128]
-
+                at, col = (tx * 4 + 2 + sy - 2 * ty) * 256, (tx * 2 + ty) * 128
+                mine[sx, at : at + 256] = result[:, col : col + 128]
+
+    middle(back)
+    finish(gp_copies)
+    clear_outside(gpf)
+    ends_along(back, 1, 2)
+    ends_along(back, 3, 4)
+    ends_across(back, 3)
+    conv_sum.step1()
     up_grad(0, 0)
     up_grad(0, 1)
-    sums.step0(0)
+    even.step0()
+    ends_along(back, 2, 3)
+    ends_along(back, 0, 1)
+    ends_across(back, 0)
+    even.step1()
     up_grad(1, 0)
     up_grad(1, 1)
-    sums.step0(1)
+    odd.step0()
+    conv_sum.step2()
 
     acc[...] = jnp.zeros_like(acc)
 
@@ -638,11 +634,12 @@
 
     lower(0, 0)
     lower(1, 0)
-    sums.step1()
     lower(0, 1)
+    odd.step1()
     lower(1, 1)
     lower(0, 2)
     lower(1, 2)
+    even.step2()
 
     def turned(i, y):
         return acc[i, y].T
@@ -665,7 +662,8 @@
     lax.fori_loop(0, 6, fold, 0)
     part_copies = halo_copies(part, part_in, halo_send, halo_recv, 32, padding)
     start(part_copies)
-    sums.step2()
+    conv_sum.step3()
+    odd.step2()
 
     def turn_feat(x, carry):
         feat_t[:, x] = jnp.swapaxes(feat[x], 0, 1)
@@ -677,7 +675,8 @@
         pltpu.make_async_copy(gs_t, gs_any, local_sem.at[4]),
     ]
     start(stores[0:1])
-    sums.step3()
+    even.step3()
+    odd.step3()
 
     def turn_gs(x, carry):
         gs_t[:, x] = jnp.swapaxes(gs[x], 0, 1)
@@ -685,7 +684,9 @@
 
     lax.fori_loop(0, 8, turn_gs, 0, unroll=2)
     start(stores[1:2])
-    sums.step4()
+    conv_sum.step4()
+    even.step4()
+    odd.step4()
     finish(part_copies)
     clear_outside(part_in)
     for x in range(4):
@@ -698,8 +699,13 @@
                     if (px, py) != (x + 1, y + 1):
                         value += part_in[px, py].astype(F32)
             low[x, y] = jnp.where(keep_ref[...] > 0.5, value, 0.0).astype(BF)
+    conv_sum.step5()
+    even.step5()
+    odd.step5()
     finish(stores)
-    sums.step5()
+    conv_sum.step6()
+    even.step6()
+    odd.step6()
 
 
 def final_body(
@@ -725,9 +731,9 @@
     def part(at, count):
         return total.at[pl.ds(at, count)], sums.at[pl.ds(at, count)]
 
-    taps = [(2 + sx - 2 * tx, tx * HALF + sx * SUB) for tx in range(2) for sx in range(2)]
-    pieces = [part(2 * SUB, C_ROWS), part(HALF + 2 * SUB, C_ROWS)]
-    pieces += [part(at, SUB) for kx, at in taps]
+    taps = [(2 + sx - 2 * tx, sx * PIECE + tx * HALF) for tx in range(2) for sx in range(2)]
+    pieces = [part(2 * PIECE, C_ROWS), part(2 * PIECE + C_ROWS, C_ROWS)]
+    pieces += [part(at, HALF) for kx, at in taps]
     pieces += [(feat, v0), (gs, v1), (low, v2)]
     come = [pltpu.make_async_copy(a, b, come_sem.at[n]) for n, (a, b) in enumerate(pieces)]
     start(come)
@@ -736,13 +742,13 @@
     go = [pltpu.make_async_copy(a, b, go_sem.at[n]) for n, (a, b) in enumerate(go)]
     finish(come[0:2])
     for tap in range(9):
-        at = 2 * SUB + tap * 64
+        at = 2 * PIECE + tap * 64
         left = sums[at : at + 64].astype(F32) * scale
-        right = sums[HALF + at : HALF + at + 64].astype(F32) * scale
+        right = sums[C_ROWS + at : C_ROWS + at + 64].astype(F32) * scale
         conv[tap // 3, tap % 3, 0] = left[:, 0:64]
         conv[tap // 3, tap % 3, 1] = left[:, 64:128]
         conv[tap // 3, tap % 3, 2] = right[:, 0:64]
-    bias[...] = (sums[2 * SUB + 576 : 2 * SUB + 592].astype(F32) * scale)[0:1, 64:128]
+    bias[...] = (sums[2 * PIECE + 576 : 2 * PIECE + 592].astype(F32) * scale)[0:1, 64:128]
     for n, (kx, at) in enumerate(taps):
         come[2 + n].wait()
 
@@ -774,7 +780,7 @@
     plane = (64, 8, 8, 128)
     feat, gs, low, total = pl.pallas_call(
         main_body,
-        out_shape=[shape(plane), shape(plane), shape((4, 4, 64, 128)), shape((2 * HALF, 128))],
+        out_shape=[shape(plane), shape(plane), shape((4, 4, 64, 128)), shape((3, PIECE, 128))],
         in_specs=[anywhere] * 7 + [vmem] * 4,
         out_specs=[anywhere] * 2 + [vmem] * 2,
         scratch_shapes=[
@@ -811,16 +817,16 @@
             pltpu.VMEM((4, 6, 128, 128), F32),
             pltpu.VMEM((6, 6, 64, 128), BF),
             pltpu.VMEM((6, 6, 64, 128), BF),
-            pltpu.VMEM((2, 3, SUB, 128), BF),
-            pltpu.VMEM((HALF, 128), BF),
+            pltpu.VMEM((3, PIECE, 128), BF),
+            pltpu.VMEM((3, HALF, 128), BF),
+            pltpu.VMEM((3, 3, QUARTER, 128), BF),
+            pltpu.VMEM((3, 15, CHUNK, 128), BF),
             pltpu.VMEM((3, QUARTER, 128), BF),
-            pltpu.VMEM((15, CHUNK, 128), BF),
-            pltpu.VMEM((QUARTER, 128), BF),
-            pltpu.VMEM((QUARTER, 128), BF),
+            pltpu.VMEM((3, QUARTER, 128), BF),
             pltpu.SemaphoreType.DMA((40,)),
             pltpu.SemaphoreType.DMA((40,)),
-            pltpu.SemaphoreType.DMA((43,)),
-            pltpu.SemaphoreType.DMA((43,)),
+            pltpu.SemaphoreType.DMA((3 * 38,)),
+            pltpu.SemaphoreType.DMA((3 * 38,)),
         ],
         compiler_params=pltpu.CompilerParams(
             vmem_limit_bytes=LIMIT, collective_id=1, has_side_effects=True
@@ -855,13 +861,13 @@
             pltpu.VMEM(plane, BF),
             pltpu.VMEM(plane, BF),
             pltpu.VMEM((4, 4, 64, 128), BF),
-            pltpu.VMEM((2 * HALF, 128), BF),
+            pltpu.VMEM((3 * PIECE, 128), BF),
             pltpu.VMEM((4, 4, 4, 64, 128), F32),
             pltpu.SemaphoreType.DMA((9,)),
             pltpu.SemaphoreType.DMA((7,)),
         ],
         compiler_params=pltpu.CompilerParams(vmem_limit_bytes=LIMIT),
-    )(feat, gs, low, total)
+    )(feat, gs, low, total.reshape(3 * PIECE, 128))
     grad_coarse = jnp.transpose(low, (3, 0, 1, 2))
     grad_up = jnp.transpose(up, (0, 1, 2, 4, 3))
     return features, grad_skip, grad_coarse, grad_up, grad_conv, bias[0]

time: 90.8 us -> 83.6 us (0.921)
  Pallas kernels: 89.8 us -> 82.6 us
    pallas_call x1, Pallas kernels: 85.5 us -> 78.3 us  [body(): pl.pallas_call(main_body, out_shape=[shape(plane), shape(plane), shape((4...]
where the time goes in v5:
time: 83.6 us; the launch traced here: 83.4 us
  Pallas kernels  82.6 us (99%)
    pallas_call x1, Pallas kernels, body(): pl.pallas_call(main_body, out_shape=[shape(plane), shape(plane), shape((4...  78.3 us
    pallas_call x1, Pallas kernels, body(): pl.pallas_call(functools.partial(final_body, float(cells) ** (-0.5)), out...  4.34 us

profile of v5, /device:TPU:1, one launch (start us, length us, event | category | flops | bytes accessed | tf_op | source)
XLA Modules:
  0.0 83.4 jit_solution(1699118558011826825)
XLA Ops:
  0.6 78.3 %shard_map.154 = (bf16[64,8,8,128]{3,2,1,0:T(8,128)(2,1)}, bf16[64,8,8,128]{3,2,1,0:T(8,128)(2,1)}, bf16[4,4,64,128]{3,2,1,0:T(8,128)(2,1)}, bf16[3,2048,128]{2,1,0:T(8,128)(2,1)}) custom-call(bf16[64,8,8,128]{3,2,1,0:T(8,128)(2,1)} %skip_any.1, bf16[64,8,8,128]{3,2,1,0:T(8,128)(2,1)} %cot_any.1, bf16[4,4,4,64,128]{4,3,2,1,0:T(8,128)(2,1)} %bitcast.9, ...), custom_call_target="tpu_custom_call" | custom-call | tf_op jit(solution)/shard_map/pallas_call | solution.py:781
  78.9 4.3 %shard_map.155 = (bf16[64,8,8,128]{3,2,1,0:T(8,128)(2,1)}, bf16[64,8,8,128]{3,2,1,0:T(8,128)(2,1)}, bf16[4,4,64,128]{3,2,1,0:T(8,128)(2,1)}, f32[4,4,4,64,128]{4...) custom-call(bf16[64,8,8,128]{3,2,1,0:T(8,128)(2,1)} %get-tuple-element.16.feat, ...), custom_call_target="tpu_custom_call" | custom-call | tf_op jit(solution)/shard_map/pallas_call | solution.py:848

commit v6 on v5

--- a/solution.py
+++ b/solution.py
@@ -94,6 +94,19 @@
         copy.wait()
 
 
+def clear_across(field):
+    across, along = field.shape[0], field.shape[1]
+    row = jnp.zeros((1, along - 2) + field.shape[2:], field.dtype)
+
+    @pl.when(lax.axis_index("gx") == 0)
+    def _():
+        field[0:1, 1 : along - 1] = row
+
+    @pl.when(lax.axis_index("gx") == lax.axis_size("gx") - 1)
+    def _():
+        field[across - 1 : across, 1 : along - 1] = row
+
+
 def clear_outside(field):
     across, along = field.shape[0], field.shape[1]
     nx, ny = lax.axis_size("gx"), lax.axis_size("gy")
@@ -144,9 +157,21 @@
         y = jnp.where(self.core == 0, a, self.y)
         return a * 4 + b, self.device(x, y, b, self.core)
 
+    def across_first(self, step):
+        x = jnp.where(self.core == 0, self.x, lax.rem(self.x + step, 4))
+        y = jnp.where(self.core == 0, lax.rem(self.y + step, 4), self.y)
+        return self.device(x, y, self.z, 1 - self.core)
+
+    def beside_first(self, step):
+        other = lax.rem(self.first + step, 4)
+        x = jnp.where(self.core == 0, other, self.x)
+        y = jnp.where(self.core == 0, self.y, other)
+        return self.device(x, y, self.z, 1 - self.core)
+
     def greet(self, barrier):
         partners = [self.twin]
         partners += [self.along_first(step)[1] for step in range(1, 4)]
+        partners += [self.across_first(step) for step in range(1, 4)]
         partners += [self.in_plane(step)[1] for step in range(1, 16)]
         for partner in partners:
             pl.semaphore_signal(barrier, inc=1, device_id=partner, device_id_type=MESH)
@@ -158,8 +183,8 @@
 
 
 class Piece:
-    def __init__(self, ring, index, mine, got0, got1, got2, acc1, acc2, out, send, recv):
-        self.ring, self.base = ring, index * 38
+    def __init__(self, ring, index, wide, mine, got0, got1, got2, acc1, acc2, out, send, recv):
+        self.ring, self.base, self.wide = ring, index * 42, wide
         self.mine, self.got0, self.got1 = mine.at[index], got0.at[index], got1.at[index]
         self.got2, self.acc1, self.acc2 = got2.at[index], acc1.at[index], acc2.at[index]
         self.out, self.send, self.recv = out.at[index], send, recv
@@ -238,6 +263,11 @@
         for step in range(1, 4):
             other, to = ring.along_first(step)
             copies.append(self.remote(self.acc2, self.out.at[own], 33 + step, to))
+            if self.wide:
+                to = ring.beside_first(step)
+                copies.append(self.remote(self.acc2, self.out.at[own], 36 + step, to))
+        if self.wide:
+            copies.append(self.remote(self.acc2, self.out.at[own], 40, ring.twin))
         self.launch(copies)
         self.out[own] = self.acc2[...]
 
@@ -290,6 +320,8 @@
     wide_columns,
     feat_any,
     gs_any,
+    low_any,
+    total_any,
     low,
     total,
     skip,
@@ -388,7 +420,6 @@
         return carry
 
     lax.fori_loop(0, 8, fill_cot, 0, unroll=2)
-    start(skip_copies)
     finish(loads[3:7])
     bias[...] = jnp.broadcast_to(conv_bias[...], (128, 64)).T
     for kz in range(3):
@@ -444,6 +475,7 @@
         for at, (p, q) in enumerate(blocks):
             join(p, q, taps[:, at * 128 : at * 128 + 128])
 
+    start(skip_copies)
     lax.fori_loop(0, 8, pair_middle, 0, unroll=4)
     upsample([(1, 1), (1, 2), (1, 3)])
     finish(coarse_copies)
@@ -472,11 +504,11 @@
         return carry
 
     def mix_across(t, carry):
-        mix((t // 10) * 9, t % 10)
+        mix((t // 8) * 9, 1 + t % 8)
         return carry
 
     def mix_along(t, carry):
-        mix(1 + t // 2, (t % 2) * 9)
+        mix(t // 2, (t % 2) * 9)
         return carry
 
     lax.fori_loop(0, 64, mix_middle, 0, unroll=4)
@@ -526,8 +558,8 @@
     gp_copies = halo_copies(gpf, gpf, halo_send, halo_recv, 24)
     middle(conv)
     finish(skip_copies)
-    lax.fori_loop(0, 20, mix_across, 0, unroll=4)
-    lax.fori_loop(0, 16, mix_along, 0, unroll=4)
+    lax.fori_loop(0, 16, mix_across, 0, unroll=4)
+    lax.fori_loop(0, 20, mix_along, 0, unroll=4)
     ends_along(conv, 0, 4)
     start(gp_copies[0:2])
     start(gp_copies[4:8])
@@ -558,7 +590,7 @@
     mine[2, C_ROWS : 2 * C_ROWS, 64:128] = jnp.zeros((C_ROWS, 64), BF)
     mine[2, 2 * C_ROWS : PIECE] = jnp.zeros((PIECE - 2 * C_ROWS, 128), BF)
     sums = [
-        Piece(ring, at, mine, got0, got1, got2, acc1, acc2, total, sum_send, sum_recv)
+        Piece(ring, at, at == 1, mine, got0, got1, got2, acc1, acc2, total, sum_send, sum_recv)
         for at in range(3)
     ]
     even, odd, conv_sum = sums
@@ -687,6 +719,13 @@
     conv_sum.step4()
     even.step4()
     odd.step4()
+    stores.append(pltpu.make_async_copy(low, low_any, local_sem.at[9]))
+    stores += [
+        pltpu.make_async_copy(total.at[at], total_any.at[at], local_sem.at[10 + at])
+        for at in range(3)
+    ]
+    conv_sum.step5()
+    even.step5()
     finish(part_copies)
     clear_outside(part_in)
     for x in range(4):
@@ -699,13 +738,14 @@
                     if (px, py) != (x + 1, y + 1):
                         value += part_in[px, py].astype(F32)
             low[x, y] = jnp.where(keep_ref[...] > 0.5, value, 0.0).astype(BF)
-    conv_sum.step5()
-    even.step5()
-    odd.step5()
+    stores[2].start()
+    conv_sum.step6()
+    stores[5].start()
+    even.step6()
+    stores[3].start()
+    odd.step6()
+    stores[4].start()
     finish(stores)
-    conv_sum.step6()
-    even.step6()
-    odd.step6()
 
 
 def final_body(
@@ -732,15 +772,28 @@
         return total.at[pl.ds(at, count)], sums.at[pl.ds(at, count)]
 
     taps = [(2 + sx - 2 * tx, sx * PIECE + tx * HALF) for tx in range(2) for sx in range(2)]
-    pieces = [part(2 * PIECE, C_ROWS), part(2 * PIECE + C_ROWS, C_ROWS)]
+    pieces = [(feat, v0), (gs, v1), (low, v2)]
     pieces += [part(at, HALF) for kx, at in taps]
-    pieces += [(feat, v0), (gs, v1), (low, v2)]
+    pieces += [part(2 * PIECE, C_ROWS), part(2 * PIECE + C_ROWS, C_ROWS)]
     come = [pltpu.make_async_copy(a, b, come_sem.at[n]) for n, (a, b) in enumerate(pieces)]
     start(come)
     go = [(v0, features), (v1, grad_skip), (v2, grad_coarse)]
     go += [(up.at[kx], up_any.at[kx]) for kx, at in taps]
     go = [pltpu.make_async_copy(a, b, go_sem.at[n]) for n, (a, b) in enumerate(go)]
-    finish(come[0:2])
+    for n in range(3):
+        come[n].wait()
+        go[n].start()
+    for n, (kx, at) in enumerate(taps):
+        come[3 + n].wait()
+
+        def column(t, carry):
+            block = sums[pl.ds(pl.multiple_of(at + t * 256, 256), 256)]
+            up[kx, t] = (block.astype(F32) * scale).reshape(4, 64, 128)
+            return carry
+
+        lax.fori_loop(0, 4, column, 0)
+        go[3 + n].start()
+    finish(come[7:9])
     for tap in range(9):
         at = 2 * PIECE + tap * 64
         left = sums[at : at + 64].astype(F32) * scale
@@ -749,19 +802,6 @@
         conv[tap // 3, tap % 3, 1] = left[:, 64:128]
         conv[tap // 3, tap % 3, 2] = right[:, 0:64]
     bias[...] = (sums[2 * PIECE + 576 : 2 * PIECE + 592].astype(F32) * scale)[0:1, 64:128]
-    for n, (kx, at) in enumerate(taps):
-        come[2 + n].wait()
-
-        def column(t, carry):
-            block = sums[pl.ds(pl.multiple_of(at + t * 256, 256), 256)]
-            up[kx, t] = (block.astype(F32) * scale).reshape(4, 64, 128)
-            return carry
-
-        lax.fori_loop(0, 4, column, 0)
-        go[3 + n].start()
-    for n in range(3):
-        come[6 + n].wait()
-        go[n].start()
     finish(go)
 
 
@@ -782,8 +822,10 @@
         main_body,
         out_shape=[shape(plane), shape(plane), shape((4, 4, 64, 128)), shape((3, PIECE, 128))],
         in_specs=[anywhere] * 7 + [vmem] * 4,
-        out_specs=[anywhere] * 2 + [vmem] * 2,
+        out_specs=[anywhere] * 4,
         scratch_shapes=[
+            pltpu.VMEM((4, 4, 64, 128), BF),
+            pltpu.VMEM((3, PIECE, 128), BF),
             pltpu.VMEM(plane, BF),
             pltpu.VMEM(plane, BF),
             pltpu.VMEM((4, 4, 4, 64, 128), BF),
@@ -795,7 +837,7 @@
             pltpu.VMEM((8, 8, 64, 128), BF),
             pltpu.VMEM(plane, BF),
             pltpu.VMEM(plane, BF),
-            pltpu.SemaphoreType.DMA((9,)),
+            pltpu.SemaphoreType.DMA((13,)),
             pltpu.VMEM((10, 10, 64, 128), BF),
             pltpu.VMEM((6, 6, 64, 128), BF),
             pltpu.VMEM((3, 3, 16, 128), BF),
@@ -825,8 +867,8 @@
             pltpu.VMEM((3, QUARTER, 128), BF),
             pltpu.SemaphoreType.DMA((40,)),
             pltpu.SemaphoreType.DMA((40,)),
-            pltpu.SemaphoreType.DMA((3 * 38,)),
-            pltpu.SemaphoreType.DMA((3 * 38,)),
+            pltpu.SemaphoreType.DMA((3 * 42,)),
+            pltpu.SemaphoreType.DMA((3 * 42,)),
         ],
         compiler_params=pltpu.CompilerParams(
             vmem_limit_bytes=LIMIT, collective_id=1, has_side_effects=True

time: 83.6 us -> 83.1 us (level)
  no operation moved by 1% of the time
where the time goes in v6:
time: 83.1 us; the launch traced here: 82.9 us
  Pallas kernels  82.1 us (99%)
    pallas_call x1, Pallas kernels, body(): pl.pallas_call(main_body, out_shape=[shape(plane), shape(plane), shape((4...  77.8 us
    pallas_call x1, Pallas kernels, body(): pl.pallas_call(functools.partial(final_body, float(cells) ** (-0.5)), out...  4.37 us

profile of v6, /device:TPU:1, one launch (start us, length us, event | category | flops | bytes accessed | tf_op | source)
XLA Modules:
  0.0 82.9 jit_solution(1081752991545482182)
XLA Ops:
  0.6 77.8 %shard_map.154 = (bf16[64,8,8,128]{3,2,1,0:T(8,128)(2,1)}, bf16[64,8,8,128]{3,2,1,0:T(8,128)(2,1)}, bf16[4,4,64,128]{3,2,1,0:T(8,128)(2,1)}, bf16[3,2048,128]{2,1,0:T(8,128)(2,1)}) custom-call(bf16[64,8,8,128]{3,2,1,0:T(8,128)(2,1)} %skip_any.1, bf16[64,8,8,128]{3,2,1,0:T(8,128)(2,1)} %cot_any.1, bf16[4,4,4,64,128]{4,3,2,1,0:T(8,128)(2,1)} %bitcast.9, ...), custom_call_target="tpu_custom_call" | custom-call | tf_op jit(solution)/shard_map/pallas_call | solution.py:821
  78.4 4.4 %shard_map.155 = (bf16[64,8,8,128]{3,2,1,0:T(8,128)(2,1)}, bf16[64,8,8,128]{3,2,1,0:T(8,128)(2,1)}, bf16[4,4,64,128]{3,2,1,0:T(8,128)(2,1)}, f32[4,4,4,64,128]{4...) custom-call(bf16[64,8,8,128]{3,2,1,0:T(8,128)(2,1)} %get-tuple-element.16.feat, ...), custom_call_target="tpu_custom_call" | custom-call | tf_op jit(solution)/shard_map/pallas_call | solution.py:890

commit v7 on v6

--- a/solution.py
+++ b/solution.py
@@ -693,7 +693,6 @@
 
     lax.fori_loop(0, 6, fold, 0)
     part_copies = halo_copies(part, part_in, halo_send, halo_recv, 32, padding)
-    start(part_copies)
     conv_sum.step3()
     odd.step2()
 
@@ -709,6 +708,7 @@
     start(stores[0:1])
     even.step3()
     odd.step3()
+    start(part_copies)
 
     def turn_gs(x, carry):
         gs_t[:, x] = jnp.swapaxes(gs[x], 0, 1)

time: 83.1 us -> 81.5 us (0.981)
  Pallas kernels: 82.1 us -> 80.5 us
    pallas_call x1, Pallas kernels: 77.8 us -> 76.2 us  [body(): pl.pallas_call(main_body, out_shape=[shape(plane), shape(plane), shape((4...]
where the time goes in v7:
time: 81.5 us; the launch traced here: 81.3 us
  Pallas kernels  80.5 us (99%)
    pallas_call x1, Pallas kernels, body(): pl.pallas_call(main_body, out_shape=[shape(plane), shape(plane), shape((4...  76.2 us
    pallas_call x1, Pallas kernels, body(): pl.pallas_call(functools.partial(final_body, float(cells) ** (-0.5)), out...  4.37 us

profile of v7, /device:TPU:1, one launch (start us, length us, event | category | flops | bytes accessed | tf_op | source)
XLA Modules:
  0.0 81.3 jit_solution(1388072424457909602)
XLA Ops:
  0.6 76.2 %shard_map.154 = (bf16[64,8,8,128]{3,2,1,0:T(8,128)(2,1)}, bf16[64,8,8,128]{3,2,1,0:T(8,128)(2,1)}, bf16[4,4,64,128]{3,2,1,0:T(8,128)(2,1)}, bf16[3,2048,128]{2,1,0:T(8,128)(2,1)}) custom-call(bf16[64,8,8,128]{3,2,1,0:T(8,128)(2,1)} %skip_any.1, bf16[64,8,8,128]{3,2,1,0:T(8,128)(2,1)} %cot_any.1, bf16[4,4,4,64,128]{4,3,2,1,0:T(8,128)(2,1)} %bitcast.9, ...), custom_call_target="tpu_custom_call" | custom-call | tf_op jit(solution)/shard_map/pallas_call | solution.py:821
  76.8 4.4 %shard_map.155 = (bf16[64,8,8,128]{3,2,1,0:T(8,128)(2,1)}, bf16[64,8,8,128]{3,2,1,0:T(8,128)(2,1)}, bf16[4,4,64,128]{3,2,1,0:T(8,128)(2,1)}, f32[4,4,4,64,128]{4...) custom-call(bf16[64,8,8,128]{3,2,1,0:T(8,128)(2,1)} %get-tuple-element.16.feat, ...), custom_call_target="tpu_custom_call" | custom-call | tf_op jit(solution)/shard_map/pallas_call | solution.py:890

commit v8 on v7

--- a/solution.py
+++ b/solution.py
@@ -708,6 +708,7 @@
     start(stores[0:1])
     even.step3()
     odd.step3()
+    conv_sum.step4()
     start(part_copies)
 
     def turn_gs(x, carry):
@@ -716,7 +717,7 @@
 
     lax.fori_loop(0, 8, turn_gs, 0, unroll=2)
     start(stores[1:2])
-    conv_sum.step4()
+    conv_sum.step5()
     even.step4()
     odd.step4()
     stores.append(pltpu.make_async_copy(low, low_any, local_sem.at[9]))
@@ -724,7 +725,6 @@
         pltpu.make_async_copy(total.at[at], total_any.at[at], local_sem.at[10 + at])
         for at in range(3)
     ]
-    conv_sum.step5()
     even.step5()
     finish(part_copies)
     clear_outside(part_in)

time: 81.5 us -> 82.6 us (1.013)
  Pallas kernels: 80.5 us -> 81.6 us
    pallas_call x1, Pallas kernels: 76.2 us -> 77.3 us  [body(): pl.pallas_call(main_body, out_shape=[shape(plane), shape(plane), shape((4...]
where the time goes in v8:
time: 82.6 us; the launch traced here: 82.4 us
  Pallas kernels  81.6 us (99%)
    pallas_call x1, Pallas kernels, body(): pl.pallas_call(main_body, out_shape=[shape(plane), shape(plane), shape((4...  77.3 us
    pallas_call x1, Pallas kernels, body(): pl.pallas_call(functools.partial(final_body, float(cells) ** (-0.5)), out...  4.37 us

profile of v8, /device:TPU:1, one launch (start us, length us, event | category | flops | bytes accessed | tf_op | source)
XLA Modules:
  0.0 82.4 jit_solution(13660796640576300906)
XLA Ops:
  0.6 77.3 %shard_map.154 = (bf16[64,8,8,128]{3,2,1,0:T(8,128)(2,1)}, bf16[64,8,8,128]{3,2,1,0:T(8,128)(2,1)}, bf16[4,4,64,128]{3,2,1,0:T(8,128)(2,1)}, bf16[3,2048,128]{2,1,0:T(8,128)(2,1)}) custom-call(bf16[64,8,8,128]{3,2,1,0:T(8,128)(2,1)} %skip_any.1, bf16[64,8,8,128]{3,2,1,0:T(8,128)(2,1)} %cot_any.1, bf16[4,4,4,64,128]{4,3,2,1,0:T(8,128)(2,1)} %bitcast.9, ...), custom_call_target="tpu_custom_call" | custom-call | tf_op jit(solution)/shard_map/pallas_call | solution.py:821
  77.9 4.4 %shard_map.155 = (bf16[64,8,8,128]{3,2,1,0:T(8,128)(2,1)}, bf16[64,8,8,128]{3,2,1,0:T(8,128)(2,1)}, bf16[4,4,64,128]{3,2,1,0:T(8,128)(2,1)}, f32[4,4,4,64,128]{4...) custom-call(bf16[64,8,8,128]{3,2,1,0:T(8,128)(2,1)} %get-tuple-element.16.feat, ...), custom_call_target="tpu_custom_call" | custom-call | tf_op jit(solution)/shard_map/pallas_call | solution.py:890
